TPU v7x, 128 devices: a whole 4x4x4 slice. The times are simulated.
128 devices in a mesh: gz: 4 (over z), xy: 32 (over x, y, core).
Axes of the slice: x: 4, y: 4, z: 4, core: 2. Of those that a mesh axis runs over, the one named last changes fastest.
Arguments:
- volume: bfloat16 [512, 4096, 128], P('gz', 'xy'), may hold values from -6 to 6
- corners: int32 [3, 8192], P(None, ('gz', 'xy')), may hold values from 0 to 95
- destination: int32 [8192, 1], P(('gz', 'xy')), may hold values from 0 to 31; in each aligned block of 64 rows (0 to 63, 64 to 127, ...) at most 4 rows name the same one
- svx_ids: int32 [8192], P(('gz', 'xy')), may hold values from 0 to 4095
- svx_rows: int32 [4096], replicated, may hold values from 0 to 4095, each once
- stem_w: bfloat16 [3, 3, 3, 1, 64], replicated, may hold values from -1.25 to 1.25
- stem_b: float32 [64], replicated, may hold values from -3 to 3
- conv_w1: bfloat16 [3, 3, 3, 64, 64], replicated, may hold values from -0.15625 to 0.15625
- conv_b1: float32 [64], replicated, may hold values from -3 to 3
- conv_w2: bfloat16 [3, 3, 3, 64, 64], replicated, may hold values from -0.15625 to 0.15625
- conv_b2: float32 [64], replicated, may hold values from -3 to 3
- head_w: bfloat16 [64, 64], replicated, may hold values from -0.75 to 0.75
- head_b: float32 [64], replicated, may hold values from -3 to 3
Outputs:
- svx_sums: float32 [4096, 64], P('xy')
- worker_batch: float32 [16384, 64], P(('gz', 'xy'))
Inputs may be any that keep to these rules, and one draw needn't show every extreme that they name: `destination`: no more than 4 sites of one device name one worker, and exactly 4 do for some worker of some devices. `svx_rows`: each row once.
All inputs are finite; a program needn't handle non-finite values.
Results may differ from a plain program's by a relative error of at most 0.0003.
Values may be sent and summed in bfloat16 or wider, within the bound.
No kernel may reach another device: no remote copies, remote signals or barrier semaphores. Data moves between devices by JAX's collectives and lax.ppermute only.
A program may use at most 320 MiB of HBM per device.

v0:
```python
import jax
import jax.numpy as jnp
from jax import lax
from jax.sharding import PartitionSpec as P

CUT = 33


def convolve(field, kernel, stride, padding):
    return lax.conv_general_dilated(
        field,
        kernel,
        (stride, stride, stride),
        padding,
        dimension_numbers=("NDHWC", "DHWIO", "NDHWC"),
        preferred_element_type=jnp.float32,
    )


def embed(cutouts, params):
    stem_w, stem_b, conv_w1, conv_b1, conv_w2, conv_b2, head_w, head_b = params
    stem = jax.nn.relu(convolve(cutouts[..., None], stem_w, 2, "VALID") + stem_b).astype(
        jnp.bfloat16
    )
    pooled = lax.reduce_window(
        stem, jnp.array(-jnp.inf, jnp.bfloat16), lax.max, (1, 2, 2, 2, 1), (1, 2, 2, 2, 1), "VALID"
    )
    inner = jax.nn.relu(convolve(pooled, conv_w1, 1, "SAME") + conv_b1).astype(jnp.bfloat16)
    block = jax.nn.relu(convolve(inner, conv_w2, 1, "SAME") + conv_b2 + pooled.astype(jnp.float32))
    mean_act = jnp.mean(block, axis=(1, 2, 3))
    return jnp.dot(mean_act, head_w.astype(jnp.float32), precision=lax.Precision.HIGHEST) + head_b


def body(
    volume,
    corners,
    destination,
    svx_ids,
    svx_rows,
    stem_w,
    stem_b,
    conv_w1,
    conv_b1,
    conv_w2,
    conv_b2,
    head_w,
    head_b,
):
    params = (stem_w, stem_b, conv_w1, conv_b1, conv_w2, conv_b2, head_w, head_b)
    sites = corners.shape[1]
    n_xy = lax.axis_size("xy")
    cap = max(2, 2 * sites // n_xy)
    lanes = n_xy * cap
    cutouts = jax.vmap(lambda a, b, c: lax.dynamic_slice(volume, (a, b, c), (CUT, CUT, CUT)))(
        corners[0], corners[1], corners[2]
    )
    dest = destination[:, 0]
    onehot = (dest[:, None] == jnp.arange(n_xy, dtype=jnp.int32)[None, :]).astype(jnp.int32)
    rank = jnp.sum((jnp.cumsum(onehot, axis=0) - onehot) * onehot, axis=1)
    slot = dest * cap + rank
    place = slot[None, :] == jnp.arange(lanes, dtype=jnp.int32)[:, None]
    targets = jnp.take(svx_rows, svx_ids)
    own = embed(cutouts, params)
    sent = jnp.dot(place.astype(jnp.float32), own, precision=lax.Precision.HIGHEST).reshape(
        n_xy, cap, -1
    )
    worker_batch = lax.all_to_all(sent, "xy", split_axis=0, concat_axis=0, tiled=True).reshape(
        lanes, -1
    )
    sv_dev = svx_rows.shape[0] // n_xy
    hits = (
        jnp.arange(sv_dev * lax.axis_size("xy"), dtype=jnp.int32)[:, None] == targets[None, :]
    ).astype(jnp.float32)
    partial_sums = lax.psum_scatter(
        jnp.dot(hits, own, precision=lax.Precision.HIGHEST), "xy", scatter_dimension=0, tiled=True
    )
    svx_sums = lax.psum(partial_sums, "gz")
    return (svx_sums, worker_batch)


def solution(mesh):
    placed = (
        P("gz", "xy", None),
        P(None, ("gz", "xy")),
        P(("gz", "xy"), None),
        P(("gz", "xy")),
        P(),
        P(),
        P(),
        P(),
        P(),
        P(),
        P(),
        P(),
        P(),
    )
    return jax.shard_map(
        body,
        mesh=mesh,
        in_specs=placed,
        out_specs=(P("xy", None), P(("gz", "xy"), None)),
        check_vma=False,
    )
```

profile of v0, /device:TPU:0, one launch (start us, length us, event | category | flops | bytes accessed | tf_op | source)
XLA Modules:
  0.0 641.9 jit_solution(6069584247204720900)
XLA Ops:
  8.0 292.9 %while.1 = (s32[]{:T(128)}, bf16[128,128,128]{2,1,0:T(8,128)(2,1)}, s32[64,3]{0,1:T(4,128)S(1)}, bf16[64,33,33,33]{3,2,1,0:T(8,128)(2,1)}, s32[]{:T(128)}) while((s32[]{:T(128)}, bf16[128,128,128]{2,1,0:T(8,128)(2,1)}, s32[64,3]{0,1:T(4,128)S(1)}, bf16[64,33,33,33]{3,2,1,0:T(8,128)(2,1)}, s32[]{:T(128)}) %tuple.27), condition=%wide.while_cond, body=%wide.while_body.sunk | while | flops 2 | bytes 678001 | solution.py:54
  13.3 3.9 bitcast_dynamic-update-slice_fusion.2
  22.4 3.9 bitcast_dynamic-update-slice_fusion.2
  36.1 3.9 bitcast_dynamic-update-slice_fusion.2
  49.9 3.9 bitcast_dynamic-update-slice_fusion.2
  54.5 3.9 bitcast_dynamic-update-slice_fusion.2
  72.7 3.9 bitcast_dynamic-update-slice_fusion.2
  81.9 3.9 bitcast_dynamic-update-slice_fusion.2
  100.2 3.9 bitcast_dynamic-update-slice_fusion.2
  118.5 3.9 bitcast_dynamic-update-slice_fusion.2
  123.1 3.9 bitcast_dynamic-update-slice_fusion.2
  127.7 3.9 bitcast_dynamic-update-slice_fusion.2
  132.3 3.9 bitcast_dynamic-update-slice_fusion.2
  141.4 3.9 bitcast_dynamic-update-slice_fusion.2
  150.6 3.9 bitcast_dynamic-update-slice_fusion.2
  182.6 3.9 bitcast_dynamic-update-slice_fusion.2
  187.2 3.9 bitcast_dynamic-update-slice_fusion.2
  191.8 3.9 bitcast_dynamic-update-slice_fusion.2
  210.0 3.9 bitcast_dynamic-update-slice_fusion.2
  232.9 3.9 bitcast_dynamic-update-slice_fusion.2
  237.5 3.9 bitcast_dynamic-update-slice_fusion.2
  274.1 3.9 bitcast_dynamic-update-slice_fusion.2
  287.8 3.9 bitcast_dynamic-update-slice_fusion.2
  297.0 3.9 bitcast_dynamic-update-slice_fusion.2
  300.9 66.6 %copy.17 = bf16[64,33,33,33,1]{0,4,3,2,1:T(2,128)(2,1)} copy(bf16[64,33,33,33,1]{3,2,1,0,4:T(8,128)(2,1)} %bitcast.32) | data formatting | bytes 9199872 | tf_op jit(solution)/shard_map/broadcast_in_dim | solution.py:22
  368.8 54.3 %fusion.10 = f32[64,16,16,16,64]{4,0,3,2,1:T(8,128)} fusion(bf16[64,33,33,33,1]{0,4,3,2,1:T(2,128)(2,1)} %copy.17, bf16[3,3,3,1,64]{4,2,3,1,0:T(4,128)(2,1)S(1)} %copy-done.11), kind=kOutput, calls=%fused_computation.21 | convolution fusion | flops 905969664 | bytes 71712256 | tf_op jit(solution)/shard_map/conv_general_dilated | solution.py:10
  423.2 45.2 %fusion = bf16[64,8,8,8,64]{4,0,3,2,1:T(8,128)(2,1)} fusion(f32[64,16,16,16,64]{4,0,3,2,1:T(8,128)} %fusion.10, f32[64]{0:T(128)S(1)} %copy-done.10), kind=kOutput, calls=%fused_computation.4 | output fusion | flops 65011712 | bytes 71303424 | tf_op jit(solution)/shard_map/reduce_window | solution.py:25
  468.4 33.6 %maximum_convert_fusion.2 = bf16[64,8,8,8,64]{4,0,3,2,1:T(8,128)(2,1)S(1)} fusion(bf16[64,8,8,8,64]{4,0,3,2,1:T(8,128)(2,1)} %fusion, bf16[3,3,3,64,64]{4,3,2,1,0:T(8,128)(2,1)S(1)} %copy-done, f32[64]{0:T(128)S(1)} %copy-done.4), kind=kOutput, calls=%fused_computation.8 | convolution fusion | flops 5588910080 | bytes 8610048 | tf_op jit(solution)/shard_map/conv_general_dilated | solution.py:10
  502.1 31.8 %maximum_reduce_fusion = f32[64,64]{1,0:T(8,128)S(1)} fusion(bf16[64,8,8,8,64]{4,0,3,2,1:T(8,128)(2,1)S(1)} %copy-done.1, bf16[64,8,8,8,64]{4,0,3,2,1:T(8,128)(2,1)S(1)} %maximum_convert_fusion.2, bf16[3,3,3,64,64]{4,3,2,1,0:T(8,128)(2,1)S(1)} %copy-done.3, f32[64]{0:T(128)S(1)} %copy-done.5), kind=kOutput, calls=%fused_computation.7 | convolution fusion | flops 5593100288 | bytes 8626432 | tf_op jit(solution)/shard_map/conv_general_dilated | solution.py:10
  537.1 14.6 %all_to_all.5 = f32[32,1,256]{2,1,0:T(1,128)S(1)} all-to-all(f32[32,1,256]{2,1,0:T(1,128)S(1)} %reshape.149), channel_id=1, replica_groups=mesh['gz'=4,'xy'=32] {'xy'}, dimensions={0} | all-to-all | bytes 65536 | tf_op jit(solution)/shard_map/all_to_all | solution.py:67
  553.7 62.8 %reduce-scatter.2.cloned.1.call-done = f32[128,64]{0,1:T(8,128)} async-done(((f32[4096,64]{0,1:T(8,128)}), f32[128,64]{0,1:T(8,128)}) %reduce-scatter.2.cloned.1.call-update) | async-done | bytes 32784 | tf_op jit(solution)/shard_map/reduce_scatter | solution.py:74
  616.5 18.5 %psum.7 = f32[128,64]{0,1:T(8,128)} all-reduce(f32[128,64]{0,1:T(8,128)} %reduce-scatter.2.cloned.1.call-done), channel_id=1, replica_groups=mesh['gz'=4,'xy'=32] {'gz'}, use_global_device_ids=true, to_apply=%region_3.4 | all-reduce | flops 8192 | bytes 65536 | tf_op jit(solution)/shard_map/psum | solution.py:77
  (216 shorter events, 209.9 us)
Async XLA Ops:
  7.2 461.2 %copy-start = (bf16[3,3,3,64,64]{4,3,2,1,0:T(8,128)(2,1)S(1)}, bf16[3,3,3,64,64]{4,3,2,1,0:T(8,128)(2,1)}, u32[]{:S(2)}) copy-start(bf16[3,3,3,64,64]{4,3,2,1,0:T(8,128)(2,1)} %param.20) | copy-start | bytes 663556
  7.2 609.4 %reduce-scatter.2.cloned.1.call-start = ((), (), s32[]{:S(2)}) async-start(), calls=%async_computation.2 | async-start | bytes 1081344 | tf_op jit(solution)/shard_map/reduce_scatter | solution.py:74
  300.9 66.6 %copy-start.12 = (s32[64]{0:T(128)S(1)}, s32[64]{0:T(128)}, u32[]{:S(2)}) copy-start(s32[64]{0:T(128)} %param.16) | copy-start | bytes 772
  300.9 66.6 %copy-start.2 = (s32[4096]{0:T(1024)S(1)}, s32[4096]{0:T(1024)}, u32[]{:S(2)}) copy-start(s32[4096]{0:T(1024)} %param.17) | copy-start | bytes 49156
  300.9 67.9 %copy-start.11 = (bf16[3,3,3,1,64]{4,2,3,1,0:T(4,128)(2,1)S(1)}, bf16[3,3,3,1,64]{4,2,3,1,0:T(4,128)(2,1)}, u32[]{:S(2)}) copy-start(bf16[3,3,3,1,64]{4,2,3,1,0:T(4,128)(2,1)} %param.18) | copy-start | bytes 10372
  368.8 54.3 %copy-start.10 = (f32[64]{0:T(128)S(1)}, f32[64]{0:T(128)}, u32[]{:S(2)}) copy-start(f32[64]{0:T(128)} %param.19) | copy-start | bytes 772
  423.2 45.2 %copy-start.4 = (f32[64]{0:T(128)S(1)}, f32[64]{0:T(128)}, u32[]{:S(2)}) copy-start(f32[64]{0:T(128)} %param.21) | copy-start | bytes 772
  468.4 33.6 %copy-start.1 = (bf16[64,8,8,8,64]{4,0,3,2,1:T(8,128)(2,1)S(1)}, bf16[64,8,8,8,64]{4,0,3,2,1:T(8,128)(2,1)}, u32[]{:S(2)}) copy-start(bf16[64,8,8,8,64]{4,0,3,2,1:T(8,128)(2,1)} %fusion) | copy-start | bytes 12582916
  468.4 33.6 %copy-start.3 = (bf16[3,3,3,64,64]{4,3,2,1,0:T(8,128)(2,1)S(1)}, bf16[3,3,3,64,64]{4,3,2,1,0:T(8,128)(2,1)}, u32[]{:S(2)}) copy-start(bf16[3,3,3,64,64]{4,3,2,1,0:T(8,128)(2,1)} %param.22) | copy-start | bytes 663556
  468.4 33.6 %copy-start.5 = (f32[64]{0:T(128)S(1)}, f32[64]{0:T(128)}, u32[]{:S(2)}) copy-start(f32[64]{0:T(128)} %param.23) | copy-start | bytes 772
  502.0 31.8 %copy-start.6 = (bf16[64,64]{1,0:T(8,128)(2,1)S(1)}, bf16[64,64]{1,0:T(8,128)(2,1)}, u32[]{:S(2)}) copy-start(bf16[64,64]{1,0:T(8,128)(2,1)} %param.24) | copy-start | bytes 24580
  502.0 31.8 %copy-start.8 = (f32[64]{0:T(128)S(1)}, f32[64]{0:T(128)}, u32[]{:S(2)}) copy-start(f32[64]{0:T(128)} %param.25) | copy-start | bytes 772
  502.0 32.0 %copy-start.9 = (s32[64]{0:T(128)S(1)}, s32[64]{0:T(128)}, u32[]{:S(2)}) copy-start(s32[64]{0:T(128)} %and_select_fusion) | copy-start | bytes 772
  502.0 34.4 %copy-start.7 = (s32[64,1]{0,1:T(1,128)S(1)}, s32[64,1]{0,1:T(1,128)}, u32[]{:S(2)}) copy-start(s32[64,1]{0,1:T(1,128)} %param.15) | copy-start | bytes 772
Sparse Core Ops, SparseCore 0:
  536.5 79.9 reduce-scatter.1
where the time goes:
time: 648 us; the launch traced here: 642 us
  local copies, waits for them, and re-layouts  362 us (56%)
  matrix products  122 us (19%)
  waiting for transfers between devices  62.8 us (10%)
  other arithmetic  47.6 us (7%)
  blocking collectives  33.1 us (5%)
  between operations  14.2 us (2%)
    gather x192, local copies, waits for them, and re-layouts  293 us
    conv_general_dilated x3, matrix products, convolve(): lax.conv_general_dilated(field, kernel, (stride, stride, stride), padding...  120 us
    broadcast_in_dim x1, local copies, waits for them, and re-layouts, embed(): cutouts[..., None]  66.6 us
    reduce_scatter x1, waiting for transfers between devices, body(): lax.psum_scatter(jnp.dot(hits, own, precision=lax.Precision.HIGHEST), 'xy...  62.8 us
    another operation x1, other arithmetic, embed(): lax.reduce_window(stem, jnp.array(-jnp.inf, jnp.bfloat16), lax.max, (1, 2...  45.2 us
    psum x1, blocking collectives, body(): svx_sums = lax.psum(partial_sums, 'gz')  18.5 us
    all_to_all x1, blocking collectives, body(): lax.all_to_all(sent, 'xy', split_axis=0, concat_axis=0, tiled=True)  14.6 us
  transfers between devices with their start and end apart: 1, of which 1 were waited for; matrix products, arithmetic and copies ran while one was open for 0% of the time, Pallas kernels for 0%

commit v1 on v0

v1 whole, which is shorter than its diff:
```python
import functools
import jax
import jax.numpy as jnp
from jax import lax
from jax.experimental import pallas as pl
from jax.experimental.pallas import tpu as pltpu
from jax.sharding import PartitionSpec as P

F32, BF16 = jnp.float32, jnp.bfloat16
STEP = 17


def lanes_of(shape):
    return lax.broadcasted_iota(jnp.int32, shape, len(shape) - 1)


def toeplitz(w_ref, big_ref):
    zero = jnp.zeros((64, 64), BF16)
    for dz in range(3):
        for xi in range(4):
            for xo in range(2):
                dx = xi - xo
                if 0 <= dx <= 2:
                    w = [w_ref[(dz * 3 + dx) * 3 + dy] for dy in range(3)]
                    rows = [(w[1], w[0]), (w[2], w[1]), (w[0], zero), (zero, w[2])]
                    tile = jnp.concatenate([jnp.concatenate(r, axis=1) for r in rows], axis=0)
                else:
                    tile = jnp.zeros((256, 128), BF16)
                big_ref[dz * 4 + xi, :, xo * 128 : (xo + 1) * 128] = tile


def stem_weights(sw_ref, ws_ref):
    t = lax.broadcasted_iota(jnp.int32, (256, 32), 1)
    k = lax.broadcasted_iota(jnp.int32, (256, 32), 0)
    kz, kx, ky = t // 9, (t // 3) % 3, t % 3
    base = jnp.where(kz == 2, 128 + STEP * kx, STEP * (kz * 3 + kx)) + ky
    base = jnp.where(t < 27, base, -1000)
    taps = sw_ref[...]
    for pair in range(4):
        for par in range(2):
            cols = []
            for inner in range(2):
                sy = 4 * pair + 2 * inner + par
                hot = (k == base + 2 * sy).astype(F32).astype(BF16)
                cols.append(jnp.dot(hot, taps, preferred_element_type=F32).astype(BF16))
            at = (pair * 2 + par) * 128
            ws_ref[:, at : at + 128] = jnp.concatenate(cols, axis=1)


def kernel(sites, corners, vol, sw, sb, w1, b1, w2, b2, hw, hb, out, vf, ub, pf, pq1, pq2, ws, big1, big2, acc):
    def widen(z, c):
        vf[z] = vol[z].astype(F32)
        return c

    lax.fori_loop(0, 128, widen, 0)
    toeplitz(w1, big1)
    toeplitz(w2, big2)
    stem_weights(sw, ws)

    lane = lanes_of((16, 128))
    masks = [[lane < STEP * (j + 1) + 16 * h for j in range(5)] for h in range(2)]

    def build(site, slot):
        z0, x0, y0 = corners[0, site], corners[1, site], corners[2, site]
        shift = [lax.rem(STEP * j + 128 - y0, 128) for j in range(6)]
        for u in range(17):
            pieces = []
            for zp in range(2 if u < 16 else 1):
                for kx in range(3):
                    a = vf[z0 + 2 * u + zp, pl.ds(x0 + kx, 8, 4), :]
                    b = vf[z0 + 2 * u + zp, pl.ds(x0 + kx + 2, 8, 4), :]
                    p = jnp.concatenate([a, b], axis=0)
                    pieces.append(pltpu.roll(p, shift[zp * 3 + kx], 1))
            for h in range(2):
                v = pieces[-1]
                for j in reversed(range(len(pieces) - 1)):
                    v = jnp.where(masks[h][j], pieces[j], v)
                ub[slot, h, u] = v.astype(BF16)

    bias = jnp.concatenate([sb[...], sb[...]], axis=1)

    def stem(site, slot):
        for h in range(2):
            lhs = jnp.concatenate(
                [ub[slot, h, 0:16].reshape(256, 128), ub[slot, h, 1:17].reshape(256, 128)], axis=1
            )
            r = jnp.dot(lhs, ws[:, h * 512 : h * 512 + 512], preferred_element_type=F32)
            r = r.reshape(8, 4, 8, 512)
            m = jnp.maximum(jnp.maximum(r[:, 0], r[:, 1]), jnp.maximum(r[:, 2], r[:, 3]))
            for pair in range(2):
                v = jnp.maximum(m[:, :, pair * 256 : pair * 256 + 128], m[:, :, pair * 256 + 128 : pair * 256 + 256])
                v = jnp.maximum(v + bias[None], 0.0)
                for z in range(8):
                    pf[z, h * 2 + pair, pl.ds(site, 8, sites), :] = v[z]

    build(0, 0)

    def both(i, c):
        s = 2 * i
        build(s + 1, 1)
        stem(s, 0)
        build(jnp.minimum(s + 2, sites - 1), 0)
        stem(s + 1, 1)
        return c

    lax.fori_loop(0, sites // 2, both, 0)

    low = lanes_of((sites, 128)) < 64

    def halo(r):
        out = []
        zero = jnp.zeros((sites, 128), F32)
        for p in range(4):
            left = r[p - 1] if p > 0 else zero
            right = r[p + 1] if p < 3 else zero
            out.append(jnp.where(low, left, right))
        return out

    def pack(z, c):
        for x in range(8):
            v = [pf[z, p, x * sites : (x + 1) * sites, :] for p in range(4)]
            q = halo([pltpu.roll(t, 64, 1) for t in v])
            for p in range(4):
                pq1[z, x, p, :, 0:128] = v[p].astype(BF16)
                pq1[z, x, p, :, 128:256] = q[p].astype(BF16)
        return c

    lax.fori_loop(0, 8, pack, 0)

    def conv(src, big, z, dzs, xb):
        xis = [xi for xi in range(4) if 0 <= 2 * xb - 1 + xi < 8]
        total = None
        for dz in dzs:
            for xi in xis:
                lhs = src[z + dz - 1, 2 * xb - 1 + xi].reshape(4 * sites, 256)
                part = jnp.dot(lhs, big[dz * 4 + xi], preferred_element_type=F32)
                total = part if total is None else total + part
        return total

    bias1 = jnp.concatenate([b1[...]] * 4, axis=1)
    bias2 = jnp.concatenate([b2[...]] * 4, axis=1)

    def first(z, dzs):
        for xb in range(4):
            v = jnp.maximum(conv(pq1, big1, z, dzs, xb) + bias1, 0.0).reshape(4, sites, 256)
            for xo in range(2):
                t = [v[p, :, xo * 128 : xo * 128 + 128] for p in range(4)]
                q = halo([pltpu.roll(s, 64, 1) for s in t])
                for p in range(4):
                    pq2[z, 2 * xb + xo, p, :, 0:128] = t[p].astype(BF16)
                    pq2[z, 2 * xb + xo, p, :, 128:256] = q[p].astype(BF16)

    def second(z, dzs):
        for xb in range(4):
            v = conv(pq2, big2, z, dzs, xb) + bias2
            skip = jnp.concatenate([pq1[z, 2 * xb + xo, :, :, 0:128].reshape(4 * sites, 128) for xo in range(2)], axis=1)
            v = jnp.maximum(v + skip.astype(F32), 0.0).reshape(4, sites, 256)
            acc[...] += jnp.sum(v, axis=0)

    def over_z(step):
        step(0, (1, 2))
        lax.fori_loop(1, 7, lambda z, c: (step(z, (0, 1, 2)), c)[1], 0)
        step(7, (0, 1))

    over_z(first)
    acc[...] = jnp.zeros_like(acc)
    over_z(second)
    a = acc[...]
    mean = (a[:, 0:64] + a[:, 64:128] + a[:, 128:192] + a[:, 192:256]) * (1.0 / 512.0)
    own = jnp.dot(mean, hw[...].astype(F32), precision=lax.Precision.HIGHEST, preferred_element_type=F32) + hb[...]
    out[...] = jnp.concatenate([own[0 : sites // 2], own[sites // 2 :]], axis=1)


def embed(volume, corners, stem_w, stem_b, conv_w1, conv_b1, conv_w2, conv_b2, head_w, head_b):
    sites = corners.shape[1]
    sw = jnp.pad(stem_w.reshape(27, 64), ((0, 5), (0, 0)))
    vmem = pl.BlockSpec(memory_space=pltpu.VMEM)
    smem = pl.BlockSpec(memory_space=pltpu.SMEM)
    return pl.pallas_call(
        functools.partial(kernel, sites),
        out_shape=jax.ShapeDtypeStruct((sites // 2, 128), F32),
        in_specs=[smem] + [vmem] * 9,
        out_specs=vmem,
        scratch_shapes=[
            pltpu.VMEM((128, 128, 128), F32),
            pltpu.VMEM((2, 2, 17, 16, 128), BF16),
            pltpu.VMEM((8, 4, 8 * sites, 128), F32),
            pltpu.VMEM((8, 8, 4, sites, 256), BF16),
            pltpu.VMEM((8, 8, 4, sites, 256), BF16),
            pltpu.VMEM((256, 1024), BF16),
            pltpu.VMEM((12, 256, 256), BF16),
            pltpu.VMEM((12, 256, 256), BF16),
            pltpu.VMEM((sites, 256), F32),
        ],
        compiler_params=pltpu.CompilerParams(vmem_limit_bytes=56 * 1024 * 1024),
        cost_estimate=pl.CostEstimate(flops=30_000_000_000, bytes_accessed=6_000_000, transcendentals=0),
    )(
        corners, volume, sw, stem_b.reshape(1, 64), conv_w1.reshape(27, 64, 64), conv_b1.reshape(1, 64),
        conv_w2.reshape(27, 64, 64), conv_b2.reshape(1, 64), head_w, head_b.reshape(1, 64),
    )


def collect_kernel(n_xy, own_rows, me_ref, codes, table, *refs):
    pieces, (batch, sums, slot, hots) = refs[:-4], refs[-4:]
    me = me_ref[0]
    wide = 2 * n_xy
    dest = codes[...]
    valid = (dest == me).astype(F32)
    earlier = (lax.broadcasted_iota(jnp.int32, (64, 64), 0) < lax.broadcasted_iota(jnp.int32, (64, 64), 1)).astype(F32)
    rank = jnp.dot(valid, earlier, preferred_element_type=F32).astype(jnp.int32)
    source = lax.broadcasted_iota(jnp.int32, (wide, 64), 0) // 2
    row = jnp.where(dest == me, source * 4 + rank, -1)
    odd = lax.broadcasted_iota(jnp.int32, (wide, 64), 0) % 2 == 1
    slot[...] = jnp.where(odd, dest, row)
    t = table[...]
    want = lax.broadcasted_iota(jnp.int32, (own_rows, 128), 0) + me * own_rows
    found = jnp.zeros((own_rows, 128), jnp.int32)
    lane = lax.broadcasted_iota(jnp.int32, (own_rows, 128), 1)
    for r in range(t.shape[0]):
        found = found + jnp.where(t[r : r + 1, :] == want, lane + r * 128, 0)
    owned = jnp.sum(found, axis=1, keepdims=True)
    rows = lax.broadcasted_iota(jnp.int32, (own_rows, 128), 0)
    for g in range(n_xy // 4):
        for half in range(2):
            lows = [[], []]
            for q in range(4 * g, 4 * g + 4):
                at = slot[pl.ds(2 * jnp.bitwise_xor(me, q), 1), :]
                aid = slot[pl.ds(2 * jnp.bitwise_xor(me, q) + 1, 1), :]
                lows[0].append(at[:, half * 32 : half * 32 + 32])
                lows[1].append(aid[:, half * 32 : half * 32 + 32])
            w, s = [jnp.concatenate(x, axis=1) for x in lows]
            top = half * 2 * own_rows
            hots[top : top + own_rows, g * 128 : g * 128 + 128] = (rows == w).astype(F32).astype(BF16)
            hots[top + own_rows : top + 2 * own_rows, g * 128 : g * 128 + 128] = (
                (owned == s).astype(F32).astype(BF16)
            )
    total = jnp.zeros((4 * own_rows, 128), F32)
    at = 0
    for p in pieces:
        x = p[...]
        hi = x.astype(BF16)
        rest = x - hi.astype(F32)
        mid = rest.astype(BF16)
        low = (rest - mid.astype(F32)).astype(BF16)
        parts = jnp.dot(
            hots[:, at : at + x.shape[0]], jnp.concatenate([hi, mid, low], axis=1), preferred_element_type=F32
        )
        total = total + (parts[:, 0:128] + (parts[:, 128:256] + parts[:, 256:384]))
        at += x.shape[0]
    n = own_rows
    batch[...] = total[0:n, 0:64] + total[2 * n : 3 * n, 64:128]
    mine = total[n : 2 * n, 0:64] + total[3 * n : 4 * n, 64:128]
    sums[...] = jnp.concatenate([mine[0 : n // 2], mine[n // 2 :]], axis=1)


def collect(pieces, codes, table, me, n_xy):
    own_rows = table.size // n_xy
    vmem = pl.BlockSpec(memory_space=pltpu.VMEM)
    return pl.pallas_call(
        functools.partial(collect_kernel, n_xy, own_rows),
        out_shape=(
            jax.ShapeDtypeStruct((own_rows, 64), F32),
            jax.ShapeDtypeStruct((own_rows // 2, 128), F32),
        ),
        in_specs=[pl.BlockSpec(memory_space=pltpu.SMEM)] + [vmem] * (2 + len(pieces)),
        out_specs=(vmem, vmem),
        scratch_shapes=[
            pltpu.VMEM((2 * n_xy, 64), jnp.int32),
            pltpu.VMEM((4 * own_rows, n_xy * 32), BF16),
        ],
        compiler_params=pltpu.CompilerParams(vmem_limit_bytes=32 * 1024 * 1024),
    )(me, codes, table, *pieces)


def body(
    volume, corners, destination, svx_ids, svx_rows,
    stem_w, stem_b, conv_w1, conv_b1, conv_w2, conv_b2, head_w, head_b,
):
    n_xy, n_gz = lax.axis_size("xy"), lax.axis_size("gz")

    def swap(a, k, axis="xy", n=n_xy):
        return lax.ppermute(a, axis, [(i, i ^ k) for i in range(n)])

    codes = lax.all_gather(jnp.stack([destination[:, 0], svx_ids]), "xy", tiled=True)
    own = embed(volume, corners, stem_w, stem_b, conv_w1, conv_b1, conv_w2, conv_b2, head_w, head_b)
    a = jnp.concatenate([own, swap(own, 1)])
    a = jnp.concatenate([a, swap(a, 2), swap(a, 4), swap(a, 6)])
    pieces = [a, swap(a, 8), swap(a, 16), swap(a, 24)]
    me = lax.axis_index("xy").astype(jnp.int32).reshape(1)
    batch, part = collect(pieces, codes, svx_rows.reshape(-1, 128), me, n_xy)
    z = [part] + [swap(part, k, "gz", n_gz) for k in (1, 2, 3)]
    total = (z[0] + z[1]) + (z[2] + z[3])
    return jnp.concatenate([total[:, 0:64], total[:, 64:128]]), batch


def solution(mesh):
    sites = P(("gz", "xy"))
    placed = (P("gz", "xy", None), P(None, ("gz", "xy")), P(("gz", "xy"), None), sites) + (P(),) * 9
    return jax.shard_map(
        body, mesh=mesh, in_specs=placed, out_specs=(P("xy", None), P(("gz", "xy"), None)), check_vma=False
    )
```

time: 648 us -> 103 us (0.16)
  local copies, waits for them, and re-layouts: 362 us -> 3.54 us
  matrix products: 122 us -> 0 us
  waiting for transfers between devices: 62.8 us -> 8.86 us
  Pallas kernels: 0 us -> 51.2 us
  other arithmetic: 47.6 us -> 0.75 us
  between operations: 14.2 us -> 0.68 us
  starting transfers between devices: 0.04 us -> 13.4 us
  blocking collectives: 33.1 us -> 23.8 us
    gather x193 -> x0, local copies, waits for them, and re-layouts: 294 us -> none
    conv_general_dilated x3 -> x0, matrix products: 120 us -> none  [convolve(): lax.conv_general_dilated(field, kernel, (stride, stride, stride), padding...]
    broadcast_in_dim x1 -> x0, local copies, waits for them, and re-layouts: 66.6 us -> none  [embed(): cutouts[..., None]]
    reduce_scatter x1 -> x0, waiting for transfers between devices: 62.8 us -> none  [body(): lax.psum_scatter(jnp.dot(hits, own, precision=lax.Precision.HIGHEST), 'xy...]
    pallas_call x0 -> x2, Pallas kernels: none -> 51.2 us  [the longest x1 50 us: embed(): pl.pallas_call(functools.partial(kernel, sites), out_shape=jax.ShapeDtype...]
    another operation x2 -> x0, other arithmetic: 45.3 us -> none  [the longest x1 45.2 us: embed(): lax.reduce_window(stem, jnp.array(-jnp.inf, jnp.bfloat16), lax.max, (1, 2...]
    all_gather x0 -> x1, blocking collectives: none -> 23.8 us  [body(): lax.all_gather(jnp.stack([destination[:, 0], svx_ids]), 'xy', tiled=True)]
    psum x1 -> x0, blocking collectives: 18.5 us -> none  [body(): svx_sums = lax.psum(partial_sums, 'gz')]
  transfers between devices with their start and end apart: 1 -> 10, of which waited for: 1 -> 5; matrix products, arithmetic and copies ran while one was open for 0% -> 1% of each run, Pallas kernels for 0% -> 0%
where the time goes in v1:
time: 103 us; the launch traced here: 102 us
  Pallas kernels  51.2 us (50%)
  blocking collectives  23.8 us (23%)
  starting transfers between devices  13.4 us (13%)
  waiting for transfers between devices  8.86 us (9%)
  local copies, waits for them, and re-layouts  3.54 us (3%)
    pallas_call x1, Pallas kernels, embed(): pl.pallas_call(functools.partial(kernel, sites), out_shape=jax.ShapeDtype...  50 us
    all_gather x1, blocking collectives, body(): lax.all_gather(jnp.stack([destination[:, 0], svx_ids]), 'xy', tiled=True)  23.8 us
    ppermute x10, starting transfers between devices, swap(): return lax.ppermute(a, axis, [(i, i ^ k) for i in range(n)])  13.4 us
    ppermute x10, waiting for transfers between devices, swap(): return lax.ppermute(a, axis, [(i, i ^ k) for i in range(n)])  8.86 us
    unnamed x12, local copies, waits for them, and re-layouts  2.13 us
  transfers between devices with their start and end apart: 10, of which 5 were waited for; matrix products, arithmetic and copies ran while one was open for 1% of the time, Pallas kernels for 0%

profile of v1, /device:TPU:0, one launch (start us, length us, event | category | flops | bytes accessed | tf_op | source)
XLA Modules:
  0.0 102.2 jit_solution(10370495131057397802)
XLA Ops:
  0.6 0.7 reshape.33
  1.3 0.6 pad.4.sw
  2.0 50.0 %shard_map.140 = f32[32,128]{1,0:T(8,128)} custom-call(s32[3,64]{1,0:T(4,128)} %corners.1, bf16[128,128,128]{2,1,0:T(8,128)(2,1)} %vol.1, bf16[32,64]{1,0:T(8,128)(2,1)} %pad.4.sw, f32[1,64]{1,0:T(1,128)} %bitcast.21, bf16[27,64,64]{2,1,0:T(8,128)(2,1)} %bitcast.19, f32[1,64]{1,0:T(1,128)} %bitcast.22, bf16[27,64,64]{2,1,0:T(8,128)(2,1)} %bitcast.20, ...), custom_call_target="tpu_custom_call" | custom-call | flops 30000001024 | bytes 6000000 | tf_op jit(solution)/shard_map/pallas_call | solution.py:179
  51.9 0.0 collective-permute-start
  51.9 0.7 constant_dynamic-update-slice_fusion.4
  52.7 0.7 collective-permute-done
  53.3 0.7 pad_maximum_fusion.1
  54.1 3.1 %collective-permute-start.3 = (f32[64,128]{1,0:T(8,128)S(1)}, f32[64,128]{1,0:T(8,128)S(1)}, u32[]{:S(2)}, u32[]{:S(2)}) collective-permute-start(f32[64,128]{1,0:T(8,128)S(1)} %pad_maximum_fusion.1), channel_id=1, source_target_pairs={{0,6},{1,7},{2,4},{3,5},{4,2},{5,3},{6,0},{7,1},{8,14},{9,15},{10,... | collective-permute-start | bytes 98312 | tf_op jit(solution)/shard_map/ppermute | solution.py:282
  57.1 0.7 collective-permute-start.2
  57.8 0.3 collective-permute-start.1
  58.2 3.6 %collective-permute-done.1 = f32[64,128]{1,0:T(8,128)S(1)} collective-permute-done((f32[64,128]{1,0:T(8,128)S(1)}, f32[64,128]{1,0:T(8,128)S(1)}, u32[]{:S(2)}, u32[]{:S(2)}) %collective-permute-start.1) | collective-permute-done | bytes 32800 | tf_op jit(solution)/shard_map/ppermute | solution.py:282
  61.7 0.8 collective-permute-done.2
  62.6 0.0 collective-permute-done.3
  62.6 2.8 %collective-permute-start.6 = (f32[256,128]{1,0:T(8,128)S(1)}, f32[256,128]{1,0:T(8,128)S(1)}, u32[]{:S(2)}, u32[]{:S(2)}) collective-permute-start(f32[256,128]{1,0:T(8,128)S(1)} %constant_dynamic-update-slice_fusion.refs_0_), channel_id=1, source_target_pairs={{0,24},{1,25},{2,26},{3,27},{4,28},{5,29},{6,30},{7,31},{8,16},{9,... | collective-permute-start | bytes 393224 | tf_op jit(solution)/shard_map/ppermute | solution.py:282
  65.4 0.9 collective-permute-start.5
  66.2 0.5 collective-permute-start.4
  66.8 0.0 copy-done.1
  66.8 0.0 copy-done.2
  66.8 23.8 %all-gather = s32[32,2,64]{2,1,0:T(2,128)S(1)} all-gather(s32[1,2,64]{2,1,0:T(2,128)S(1)} %add_bitcast_fusion), channel_id=1, replica_groups=mesh['gz'=4,'xy'=32] {'xy'}, dimensions={0}, use_global_device_ids=true | all-gather | bytes 16896 | tf_op jit(solution)/shard_map/all_gather | solution.py:284
  90.6 0.0 collective-permute-done.6.refs_3_
  90.6 0.0 collective-permute-done.5.refs_2_
  90.6 0.0 collective-permute-done.4.refs_1_
  90.6 1.2 %shard_map.141 = (f32[128,64]{1,0:T(8,128)S(1)}, f32[64,128]{1,0:T(8,128)S(1)}) custom-call(s32[1]{0:T(128)} %bitcast.me_ref, s32[64,64]{1,0:T(8,128)S(1)} %bitcast.15, s32[32,128]{1,0:T(8,128)S(1)} %bitcast.16, f32[256,128]{1,0:T(8,128)S(1)} %constant_dynamic-update-slice_fusion.refs_0_, f32[256,128]{1,0:T(8,128)S(1)} %collective-permute-done.4.refs_1_, ...), custom_call_target="tpu_custom_call" | custom-call | tf_op jit(solution)/shard_map/pallas_call | solution.py:259
  91.8 4.2 %collective-permute-start.9 = (f32[64,128]{1,0:T(8,128)S(1)}, f32[64,128]{1,0:T(8,128)S(1)}, u32[]{:S(2)}, u32[]{:S(2)}) collective-permute-start(f32[64,128]{1,0:T(8,128)S(1)} %get-tuple-element.4), channel_id=1, source_target_pairs={{0,96},{32,64},{64,32},{96,0},{1,97},{33,65},{65,33},{97,1},{2,98}... | collective-permute-start | bytes 98312 | tf_op jit(solution)/shard_map/ppermute | solution.py:282
  96.0 0.0 collective-permute-start.8
  96.0 0.9 collective-permute-start.7
  97.0 0.7 copy.18
  97.7 0.2 collective-permute-done.9
  97.9 3.5 %collective-permute-done.8 = f32[64,128]{1,0:T(8,128)S(1)} collective-permute-done((f32[64,128]{1,0:T(8,128)S(1)}, f32[64,128]{1,0:T(8,128)S(1)}, u32[]{:S(2)}, u32[]{:S(2)}) %collective-permute-start.8) | collective-permute-done | bytes 32800 | tf_op jit(solution)/shard_map/ppermute | solution.py:282
  101.4 0.0 collective-permute-done.7
  101.4 0.1 fusion
  101.5 0.7 copy.17
  (11 shorter events, 0.0 us)
Async XLA Ops:
  2.0 64.8 %copy-start.1 = (s32[64]{0:T(128)S(1)}, s32[64]{0:T(128)}, u32[]{:S(2)}) copy-start(s32[64]{0:T(128)} %param.16) | copy-start | bytes 772
  2.0 64.8 %copy-start.2 = (s32[64,1]{0,1:T(1,128)S(1)}, s32[64,1]{0,1:T(1,128)}, u32[]{:S(2)}) copy-start(s32[64,1]{0,1:T(1,128)} %param.15) | copy-start | bytes 772
  2.0 88.6 %copy-start = (s32[4096]{0:T(1024)S(1)}, s32[4096]{0:T(1024)}, u32[]{:S(2)}) copy-start(s32[4096]{0:T(1024)} %param.17) | copy-start | bytes 49156
  51.9 1.4 %collective-permute-start = (f32[32,128]{1,0:T(8,128)}, f32[32,128]{1,0:T(8,128)S(1)}, u32[]{:S(2)}, u32[]{:S(2)}) collective-permute-start(f32[32,128]{1,0:T(8,128)} %shard_map.140), channel_id=1, source_target_pairs={{0,1},{1,0},{2,3},{3,2},{4,5},{5,4},{6,7},{7,6},{8,9},{9,8},{10,11... | collective-permute-start | bytes 49160 | tf_op jit(solution)/shard_map/ppermute | solution.py:282
  54.1 8.5 %collective-permute-start.3 = (f32[64,128]{1,0:T(8,128)S(1)}, f32[64,128]{1,0:T(8,128)S(1)}, u32[]{:S(2)}, u32[]{:S(2)}) collective-permute-start(f32[64,128]{1,0:T(8,128)S(1)} %pad_maximum_fusion.1), channel_id=1, source_target_pairs={{0,6},{1,7},{2,4},{3,5},{4,2},{5,3},{6,0},{7,1},{8,14},{9,15},{10,... | collective-permute-start | bytes 98312 | tf_op jit(solution)/shard_map/ppermute | solution.py:282
  57.1 5.4 %collective-permute-start.2 = (f32[64,128]{1,0:T(8,128)S(1)}, f32[64,128]{1,0:T(8,128)S(1)}, u32[]{:S(2)}, u32[]{:S(2)}) collective-permute-start(f32[64,128]{1,0:T(8,128)S(1)} %pad_maximum_fusion.1), channel_id=1, source_target_pairs={{0,4},{1,5},{2,6},{3,7},{4,0},{5,1},{6,2},{7,3},{8,12},{9,13},{10,... | collective-permute-start | bytes 98312 | tf_op jit(solution)/shard_map/ppermute | solution.py:282
  57.8 3.9 %collective-permute-start.1 = (f32[64,128]{1,0:T(8,128)S(1)}, f32[64,128]{1,0:T(8,128)S(1)}, u32[]{:S(2)}, u32[]{:S(2)}) collective-permute-start(f32[64,128]{1,0:T(8,128)S(1)} %pad_maximum_fusion.1), channel_id=1, source_target_pairs={{0,2},{1,3},{2,0},{3,1},{4,6},{5,7},{6,4},{7,5},{8,10},{9,11},{10,... | collective-permute-start | bytes 98312 | tf_op jit(solution)/shard_map/ppermute | solution.py:282
  62.6 28.0 %collective-permute-start.6 = (f32[256,128]{1,0:T(8,128)S(1)}, f32[256,128]{1,0:T(8,128)S(1)}, u32[]{:S(2)}, u32[]{:S(2)}) collective-permute-start(f32[256,128]{1,0:T(8,128)S(1)} %constant_dynamic-update-slice_fusion.refs_0_), channel_id=1, source_target_pairs={{0,24},{1,25},{2,26},{3,27},{4,28},{5,29},{6,30},{7,31},{8,16},{9,... | collective-permute-start | bytes 393224 | tf_op jit(solution)/shard_map/ppermute | solution.py:282
  65.4 25.2 %collective-permute-start.5 = (f32[256,128]{1,0:T(8,128)S(1)}, f32[256,128]{1,0:T(8,128)S(1)}, u32[]{:S(2)}, u32[]{:S(2)}) collective-permute-start(f32[256,128]{1,0:T(8,128)S(1)} %constant_dynamic-update-slice_fusion.refs_0_), channel_id=1, source_target_pairs={{0,16},{1,17},{2,18},{3,19},{4,20},{5,21},{6,22},{7,23},{8,24},{9,... | collective-permute-start | bytes 393224 | tf_op jit(solution)/shard_map/ppermute | solution.py:282
  66.2 24.4 %collective-permute-start.4 = (f32[256,128]{1,0:T(8,128)S(1)}, f32[256,128]{1,0:T(8,128)S(1)}, u32[]{:S(2)}, u32[]{:S(2)}) collective-permute-start(f32[256,128]{1,0:T(8,128)S(1)} %constant_dynamic-update-slice_fusion.refs_0_), channel_id=1, source_target_pairs={{0,8},{1,9},{2,10},{3,11},{4,12},{5,13},{6,14},{7,15},{8,0},{9,1},... | collective-permute-start | bytes 393224 | tf_op jit(solution)/shard_map/ppermute | solution.py:282
  91.8 6.1 %collective-permute-start.9 = (f32[64,128]{1,0:T(8,128)S(1)}, f32[64,128]{1,0:T(8,128)S(1)}, u32[]{:S(2)}, u32[]{:S(2)}) collective-permute-start(f32[64,128]{1,0:T(8,128)S(1)} %get-tuple-element.4), channel_id=1, source_target_pairs={{0,96},{32,64},{64,32},{96,0},{1,97},{33,65},{65,33},{97,1},{2,98}... | collective-permute-start | bytes 98312 | tf_op jit(solution)/shard_map/ppermute | solution.py:282
  96.0 5.4 %collective-permute-start.8 = (f32[64,128]{1,0:T(8,128)S(1)}, f32[64,128]{1,0:T(8,128)S(1)}, u32[]{:S(2)}, u32[]{:S(2)}) collective-permute-start(f32[64,128]{1,0:T(8,128)S(1)} %get-tuple-element.4), channel_id=1, source_target_pairs={{0,64},{32,96},{64,0},{96,32},{1,65},{33,97},{65,1},{97,33},{2,66}... | collective-permute-start | bytes 98312 | tf_op jit(solution)/shard_map/ppermute | solution.py:282
  96.0 5.4 %collective-permute-start.7 = (f32[64,128]{1,0:T(8,128)S(1)}, f32[64,128]{1,0:T(8,128)S(1)}, u32[]{:S(2)}, u32[]{:S(2)}) collective-permute-start(f32[64,128]{1,0:T(8,128)S(1)} %get-tuple-element.4), channel_id=1, source_target_pairs={{0,32},{32,0},{64,96},{96,64},{1,33},{33,1},{65,97},{97,65},{2,34}... | collective-permute-start | bytes 98312 | tf_op jit(solution)/shard_map/ppermute | solution.py:282

commit v2 on v1

v2 whole, which is shorter than its diff:
```python
import functools
import jax
import jax.numpy as jnp
from jax import lax
from jax.experimental import pallas as pl
from jax.experimental.pallas import tpu as pltpu
from jax.sharding import PartitionSpec as P

F32, BF16 = jnp.float32, jnp.bfloat16
STEP = 17
GROUP = 16


def lanes_of(shape):
    return lax.broadcasted_iota(jnp.int32, shape, len(shape) - 1)


def toeplitz(w_ref, big_ref):
    zero = jnp.zeros((64, 64), BF16)
    for dz in range(3):
        for xi in range(4):
            for xo in range(2):
                dx = xi - xo
                if 0 <= dx <= 2:
                    w = [w_ref[(dz * 3 + dx) * 3 + dy] for dy in range(3)]
                    rows = [(w[1], w[0]), (w[2], w[1]), (w[0], zero), (zero, w[2])]
                    tile = jnp.concatenate([jnp.concatenate(r, axis=1) for r in rows], axis=0)
                else:
                    tile = jnp.zeros((256, 128), BF16)
                big_ref[dz * 4 + xi, :, xo * 128 : (xo + 1) * 128] = tile


def stem_weights(taps, ws_ref):
    t = lax.broadcasted_iota(jnp.int32, (256, 32), 1)
    k = lax.broadcasted_iota(jnp.int32, (256, 32), 0)
    kz, kx, ky = t // 9, (t // 3) % 3, t % 3
    base = jnp.where(kz == 2, 128 + STEP * kx, STEP * (kz * 3 + kx)) + ky
    base = jnp.where(t < 27, base, -1000)
    for pair in range(4):
        for par in range(2):
            cols = []
            for inner in range(2):
                sy = 4 * pair + 2 * inner + par
                hot = (k == base + 2 * sy).astype(F32).astype(BF16)
                cols.append(jnp.dot(hot, taps, preferred_element_type=F32).astype(BF16))
            at = (pair * 2 + par) * 128
            ws_ref[:, at : at + 128] = jnp.concatenate(cols, axis=1)


def kernel(sites, corners, vol, sw, sb, w1, b1, w2, b2, hw, hb, dest, ids, out, vf, ub, taps, pf0, pf1, pq1, pq2, ws, big1, big2, acc):
    def widen(z, c):
        vf[z] = vol[z].astype(F32)
        return c

    lax.fori_loop(0, 128, widen, 0)
    toeplitz(w1, big1)
    toeplitz(w2, big2)
    taps[...] = jnp.zeros_like(taps)
    for j in range(9):
        taps[3 * j : 3 * j + 3, :] = sw[j].astype(F32)
    stem_weights(taps[...].astype(BF16), ws)

    lane = lanes_of((16, 128))
    masks = [[lane < STEP * (j + 1) + 16 * h for j in range(5)] for h in range(2)]

    def build(site, slot):
        z0, x0, y0 = corners[0, site], corners[1, site], corners[2, site]
        shift = [lax.rem(STEP * j + 128 - y0, 128) for j in range(6)]
        for u in range(17):
            pieces = []
            for zp in range(2 if u < 16 else 1):
                for kx in range(3):
                    a = vf[z0 + 2 * u + zp, pl.ds(x0 + kx, 8, 4), :]
                    b = vf[z0 + 2 * u + zp, pl.ds(x0 + kx + 2, 8, 4), :]
                    p = jnp.concatenate([a, b], axis=0)
                    pieces.append(pltpu.roll(p.astype(BF16), shift[zp * 3 + kx], 1))
            for h in range(2):
                v = pieces[-1]
                for j in reversed(range(len(pieces) - 1)):
                    v = jnp.where(masks[h][j], pieces[j], v)
                ub[slot, h, u] = v

    bias = jnp.concatenate([sb[...], sb[...]], axis=1)

    def stem(pf, site, slots):
        for h in range(2):
            lhs = jnp.concatenate(
                [
                    jnp.concatenate([ub[t, h, 0:16].reshape(256, 128), ub[t, h, 1:17].reshape(256, 128)], axis=1)
                    for t in slots
                ],
                axis=0,
            )
            for pair in range(2):
                at = (h * 2 + pair) * 256
                r = jnp.dot(lhs, ws[:, at : at + 256], preferred_element_type=F32)
                r = r.reshape(len(slots), 8, 4, 8, 256)
                m = jnp.maximum(jnp.maximum(r[:, :, 0], r[:, :, 1]), jnp.maximum(r[:, :, 2], r[:, :, 3]))
                m = jnp.maximum(m[..., 0:128], m[..., 128:256])
                v = jnp.maximum(m + bias[None, None], 0.0)
                for t in range(len(slots)):
                    for z in range(8):
                        pf[z, h * 2 + pair, pl.ds(site + t, 8, GROUP + 1), :] = v[t, z]

    low = lanes_of((sites, 128)) < 64

    def halo(v, mask):
        r = [pltpu.roll(t, 64, 1) for t in v]
        zero = jnp.zeros_like(r[0])
        return [jnp.where(mask, r[p - 1] if p > 0 else zero, r[p + 1] if p < 3 else zero) for p in range(4)]

    low16 = lanes_of((GROUP, 128)) < 64

    def pack(pf, z, group):
        at = slice(group * GROUP, (group + 1) * GROUP)
        for x in range(8):
            v = [pf[z, p, x * (GROUP + 1) : x * (GROUP + 1) + GROUP, :].astype(BF16) for p in range(4)]
            q = halo(v, low16)
            for p in range(4):
                pq1[z, x, p, at, 0:128] = v[p]
                pq1[z, x, p, at, 128:256] = q[p]

    build(0, 0)
    build(1, 1)
    pfs = (pf0, pf1)
    for group in range(sites // GROUP):
        pf, done = pfs[group % 2], pfs[(group + 1) % 2]

        def four(i, c, group=group, pf=pf, done=done):
            s = group * GROUP + 4 * i
            build(s + 2, 2)
            build(s + 3, 3)
            stem(pf, 4 * i, (0, 1))
            if group > 0:
                pack(done, 2 * i, group - 1)
                pack(done, 2 * i + 1, group - 1)
            build(jnp.minimum(s + 4, sites - 1), 0)
            build(jnp.minimum(s + 5, sites - 1), 1)
            stem(pf, 4 * i + 2, (2, 3))
            return c

        lax.fori_loop(0, GROUP // 4, four, 0)

    def last(z, c):
        pack(pfs[(sites // GROUP - 1) % 2], z, sites // GROUP - 1)
        return c

    lax.fori_loop(0, 8, last, 0)

    def conv(src, big, z, dzs, xb):
        xis = [xi for xi in range(4) if 0 <= 2 * xb - 1 + xi < 8]
        total = None
        for dz in dzs:
            for xi in xis:
                lhs = src[z + dz - 1, 2 * xb - 1 + xi].reshape(4 * sites, 256)
                part = jnp.dot(lhs, big[dz * 4 + xi], preferred_element_type=F32)
                total = part if total is None else total + part
        return total

    bias1 = jnp.concatenate([b1[...]] * 4, axis=1)
    bias2 = jnp.concatenate([b2[...]] * 4, axis=1)

    def first(z, dzs):
        for xb in range(4):
            v = jnp.maximum(conv(pq1, big1, z, dzs, xb) + bias1, 0.0).reshape(4, sites, 256)
            for xo in range(2):
                t = [v[p, :, xo * 128 : xo * 128 + 128].astype(BF16) for p in range(4)]
                q = halo(t, low)
                for p in range(4):
                    pq2[z, 2 * xb + xo, p, :, 0:128] = t[p]
                    pq2[z, 2 * xb + xo, p, :, 128:256] = q[p]

    def second(z, dzs):
        for xb in range(4):
            v = conv(pq2, big2, z, dzs, xb) + bias2
            skip = jnp.concatenate([pq1[z, 2 * xb + xo, :, :, 0:128].reshape(4 * sites, 128) for xo in range(2)], axis=1)
            v = jnp.maximum(v + skip.astype(F32), 0.0).reshape(4, sites, 256)
            acc[...] += jnp.sum(v, axis=0)

    def over_z(step):
        step(0, (1, 2))
        lax.fori_loop(1, 7, lambda z, c: (step(z, (0, 1, 2)), c)[1], 0)
        step(7, (0, 1))

    over_z(first)
    acc[...] = jnp.zeros_like(acc)
    over_z(second)
    a = acc[...]
    mean = (a[:, 0:64] + a[:, 64:128] + a[:, 128:192] + a[:, 192:256]) * (1.0 / 512.0)
    own = jnp.dot(mean, hw[...].astype(F32), precision=lax.Precision.HIGHEST, preferred_element_type=F32) + hb[...]
    half = sites // 2
    out[0:half, :] = jnp.concatenate([own[0:half], own[half:]], axis=1)
    names = jnp.concatenate([dest[...].astype(F32), ids[...].astype(F32)], axis=1)
    out[half : half + 8, :] = jnp.broadcast_to(names, (8, 128))


def embed(volume, corners, destination, svx_ids, stem_w, stem_b, conv_w1, conv_b1, conv_w2, conv_b2, head_w, head_b):
    sites = corners.shape[1]
    sw = stem_w.transpose(0, 1, 3, 2, 4).reshape(9, 3, 64)
    vmem = pl.BlockSpec(memory_space=pltpu.VMEM)
    smem = pl.BlockSpec(memory_space=pltpu.SMEM)
    return pl.pallas_call(
        functools.partial(kernel, sites),
        out_shape=jax.ShapeDtypeStruct((sites // 2 + 8, 128), F32),
        in_specs=[smem] + [vmem] * 11,
        out_specs=vmem,
        scratch_shapes=[
            pltpu.VMEM((128, 128, 128), F32),
            pltpu.VMEM((4, 2, 17, 16, 128), BF16),
            pltpu.VMEM((32, 64), F32),
            pltpu.VMEM((8, 4, 8 * (GROUP + 1), 128), F32),
            pltpu.VMEM((8, 4, 8 * (GROUP + 1), 128), F32),
            pltpu.VMEM((8, 8, 4, sites, 256), BF16),
            pltpu.VMEM((8, 8, 4, sites, 256), BF16),
            pltpu.VMEM((256, 1024), BF16),
            pltpu.VMEM((12, 256, 256), BF16),
            pltpu.VMEM((12, 256, 256), BF16),
            pltpu.VMEM((sites, 256), F32),
        ],
        compiler_params=pltpu.CompilerParams(vmem_limit_bytes=56 * 1024 * 1024),
        cost_estimate=pl.CostEstimate(flops=30_000_000_000, bytes_accessed=6_000_000, transcendentals=0),
    )(
        corners, volume, sw, stem_b.reshape(1, 64), conv_w1.reshape(27, 64, 64), conv_b1.reshape(1, 64),
        conv_w2.reshape(27, 64, 64), conv_b2.reshape(1, 64), head_w, head_b.reshape(1, 64),
        destination.reshape(1, sites), svx_ids.reshape(1, sites),
    )


def collect_kernel(n_xy, own_rows, source_of, me_ref, table, *refs):
    pieces, (batch, sums, hots) = refs[:-3], refs[-3:]
    me = me_ref[0]
    size = pieces[0].shape[0]
    blocks = [(p, r) for p in pieces for r in range(0, size, 40)]
    names = jnp.concatenate([p[r + 32 : r + 33, :] for p, r in blocks], axis=0).astype(jnp.int32)
    dest, ids = names[:, 0:64], names[:, 64:128]
    valid = (dest == me).astype(F32)
    earlier = (lax.broadcasted_iota(jnp.int32, (64, 64), 0) < lax.broadcasted_iota(jnp.int32, (64, 64), 1)).astype(F32)
    rank = jnp.dot(valid, earlier, preferred_element_type=F32).astype(jnp.int32)
    source = jnp.concatenate([jnp.full((1, 64), k, jnp.int32) for k in source_of], axis=0)
    row = jnp.where(dest == me, jnp.bitwise_xor(source, me) * 4 + rank, -1)
    t = table[...]
    want = lax.broadcasted_iota(jnp.int32, (own_rows, 128), 0) + me * own_rows
    found = jnp.zeros((own_rows, 128), jnp.int32)
    lane = lax.broadcasted_iota(jnp.int32, (own_rows, 128), 1)
    for r in range(t.shape[0]):
        found = found + jnp.where(t[r : r + 1, :] == want, lane + r * 128, 0)
    owned = jnp.sum(found, axis=1, keepdims=True)
    rows = lax.broadcasted_iota(jnp.int32, (own_rows, 128), 0)
    for g in range(n_xy // 4):
        for half in range(2):
            cut = slice(half * 32, half * 32 + 32)
            w, s = [jnp.concatenate([x[q : q + 1, cut] for q in range(4 * g, 4 * g + 4)], axis=1) for x in (row, ids)]
            top = half * 2 * own_rows
            at = slice(g * 128, g * 128 + 128)
            hots[top : top + own_rows, at] = (rows == w).astype(F32).astype(BF16)
            hots[top + own_rows : top + 2 * own_rows, at] = (owned == s).astype(F32).astype(BF16)
    total = jnp.zeros((4 * own_rows, 128), F32)
    at = 0
    for p in pieces:
        x = jnp.concatenate([p[r : r + 32, :] for r in range(0, size, 40)], axis=0)
        hi = x.astype(BF16)
        rest = x - hi.astype(F32)
        mid = rest.astype(BF16)
        low = (rest - mid.astype(F32)).astype(BF16)
        parts = jnp.dot(
            hots[:, at : at + x.shape[0]], jnp.concatenate([hi, mid, low], axis=1), preferred_element_type=F32
        )
        total = total + (parts[:, 0:128] + (parts[:, 128:256] + parts[:, 256:384]))
        at += x.shape[0]
    n = own_rows
    both = [total[a : a + n, 0:64] + total[a + 2 * n : a + 3 * n, 64:128] for a in (0, n)]
    turned = jnp.concatenate(both, axis=1).T
    batch[...] = turned[0:64]
    sums[...] = turned[64:128]


def collect(pieces, source_of, table, me, n_xy):
    own_rows = table.size // n_xy
    vmem = pl.BlockSpec(memory_space=pltpu.VMEM)
    return pl.pallas_call(
        functools.partial(collect_kernel, n_xy, own_rows, source_of),
        out_shape=(jax.ShapeDtypeStruct((64, own_rows), F32),) * 2,
        in_specs=[pl.BlockSpec(memory_space=pltpu.SMEM)] + [vmem] * (1 + len(pieces)),
        out_specs=(vmem, vmem),
        scratch_shapes=[pltpu.VMEM((4 * own_rows, n_xy * 32), BF16)],
        compiler_params=pltpu.CompilerParams(vmem_limit_bytes=32 * 1024 * 1024),
    )(me, table, *pieces)


def body(
    volume, corners, destination, svx_ids, svx_rows,
    stem_w, stem_b, conv_w1, conv_b1, conv_w2, conv_b2, head_w, head_b,
):
    n_xy, n_gz = lax.axis_size("xy"), lax.axis_size("gz")

    def swap(a, k, axis="xy", n=n_xy):
        return lax.ppermute(a, axis, [(i, i ^ k) for i in range(n)])

    own = embed(
        volume, corners, destination, svx_ids, stem_w, stem_b, conv_w1, conv_b1, conv_w2, conv_b2, head_w, head_b
    )
    a = jnp.concatenate([own] + [swap(own, k) for k in (2, 4, 6)])
    pieces = [a] + [swap(a, k) for k in (8, 16, 24)]
    pieces = pieces + [swap(p, 1) for p in pieces]
    source_of = [c + x + y for c in (0, 1) for x in (0, 8, 16, 24) for y in (0, 2, 4, 6)]
    me = lax.axis_index("xy").astype(jnp.int32).reshape(1)
    batch, part = collect(pieces, source_of, svx_rows.reshape(-1, 128), me, n_xy)
    z = [part] + [swap(part, k, "gz", n_gz) for k in (1, 2, 3)]
    return ((z[0] + z[1]) + (z[2] + z[3])).T, batch.T


def solution(mesh):
    sites = P(("gz", "xy"))
    placed = (P("gz", "xy", None), P(None, ("gz", "xy")), P(("gz", "xy"), None), sites) + (P(),) * 9
    return jax.shard_map(
        body, mesh=mesh, in_specs=placed, out_specs=(P("xy", None), P(("gz", "xy"), None)), check_vma=False
    )
```

time: 103 us -> 74.9 us (0.73)
  blocking collectives: 23.8 us -> 0 us
  Pallas kernels: 51.2 us -> 44.5 us
  waiting for transfers between devices: 8.86 us -> 14.6 us
  local copies, waits for them, and re-layouts: 3.54 us -> 0.01 us
    all_gather x1 -> x0, blocking collectives: 23.8 us -> none  [body(): lax.all_gather(jnp.stack([destination[:, 0], svx_ids]), 'xy', tiled=True)]
    pallas_call x1, Pallas kernels: 50 us -> 42.3 us  [embed(): pl.pallas_call(functools.partial(kernel, sites), out_shape=jax.ShapeDtype...]
    ppermute x10 -> x13, waiting for transfers between devices: 8.86 us -> 14.6 us  [swap(): return lax.ppermute(a, axis, [(i, i ^ k) for i in range(n)])]
    unnamed x12 -> x2, local copies, waits for them, and re-layouts: 2.13 us -> 0.01 us
    ppermute x10 -> x13, starting transfers between devices: 13.4 us -> 13.6 us  [swap(): return lax.ppermute(a, axis, [(i, i ^ k) for i in range(n)])]
  transfers between devices with their start and end apart: 10 -> 13, of which waited for: 5 -> 8; matrix products, arithmetic and copies ran while one was open for 1% -> 0% of each run, Pallas kernels for 0% -> 0%
where the time goes in v2:
time: 74.9 us; the launch traced here: 74.7 us
  Pallas kernels  44.5 us (59%)
  waiting for transfers between devices  14.6 us (19%)
  starting transfers between devices  13.6 us (18%)
  other arithmetic  1.36 us (2%)
    pallas_call x1, Pallas kernels, embed(): pl.pallas_call(functools.partial(kernel, sites), out_shape=jax.ShapeDtype...  42.3 us
    ppermute x13, waiting for transfers between devices, swap(): return lax.ppermute(a, axis, [(i, i ^ k) for i in range(n)])  14.6 us
    ppermute x13, starting transfers between devices, swap(): return lax.ppermute(a, axis, [(i, i ^ k) for i in range(n)])  13.6 us
    pallas_call x1, Pallas kernels, collect(): pl.pallas_call(functools.partial(collect_kernel, n_xy, own_rows, source_o...  2.2 us
  transfers between devices with their start and end apart: 13, of which 8 were waited for; matrix products, arithmetic and copies ran while one was open for 0% of the time, Pallas kernels for 0%

profile of v2, /device:TPU:0, one launch (start us, length us, event | category | flops | bytes accessed | tf_op | source)
XLA Modules:
  0.0 74.7 jit_solution(9424957953040767442)
XLA Ops:
  0.6 0.0 copy-start
  0.6 42.3 %shard_map.140 = f32[40,128]{1,0:T(8,128)} custom-call(s32[3,64]{1,0:T(4,128)} %corners.1, bf16[128,128,128]{2,1,0:T(8,128)(2,1)} %vol.1, bf16[9,3,64]{2,1,0:T(4,128)(2,1)} %bitcast.18, f32[1,64]{1,0:T(1,128)} %bitcast.19, bf16[27,64,64]{2,1,0:T(8,128)(2,1)} %bitcast.15, f32[1,64]{1,0:T(1,128)} %bitcast.20, bf16[27,64,64]{2,1,0:T(8,128)(2,1)} %bitcast.16, ...), custom_call_target="tpu_custom_call" | custom-call | flops 30000001024 | bytes 6000000 | tf_op jit(solution)/shard_map/pallas_call | solution.py:202
  43.0 3.1 %collective-permute-start.2 = (f32[40,128]{1,0:T(8,128)}, f32[40,128]{1,0:T(8,128)S(1)}, u32[]{:S(2)}, u32[]{:S(2)}) collective-permute-start(f32[40,128]{1,0:T(8,128)} %shard_map.140), channel_id=1, source_target_pairs={{0,6},{1,7},{2,4},{3,5},{4,2},{5,3},{6,0},{7,1},{8,14},{9,15},{10,... | collective-permute-start | bytes 61448 | tf_op jit(solution)/shard_map/ppermute | solution.py:297
  46.1 0.6 collective-permute-start.1
  46.7 0.4 collective-permute-start
  47.1 1.1 %collective-permute-done.2 = f32[40,128]{1,0:T(8,128)S(1)} collective-permute-done((f32[40,128]{1,0:T(8,128)}, f32[40,128]{1,0:T(8,128)S(1)}, u32[]{:S(2)}, u32[]{:S(2)}) %collective-permute-start.2) | collective-permute-done | bytes 20512 | tf_op jit(solution)/shard_map/ppermute | solution.py:297
  48.2 3.4 %collective-permute-done.1 = f32[40,128]{1,0:T(8,128)S(1)} collective-permute-done((f32[40,128]{1,0:T(8,128)}, f32[40,128]{1,0:T(8,128)S(1)}, u32[]{:S(2)}, u32[]{:S(2)}) %collective-permute-start.1) | collective-permute-done | bytes 20512 | tf_op jit(solution)/shard_map/ppermute | solution.py:297
  51.6 0.0 collective-permute-done
  51.6 0.7 pad_maximum_fusion.refs_0_
  52.3 2.7 %collective-permute-start.5 = (f32[160,128]{1,0:T(8,128)S(1)}, f32[160,128]{1,0:T(8,128)S(1)}, u32[]{:S(2)}, u32[]{:S(2)}) collective-permute-start(f32[160,128]{1,0:T(8,128)S(1)} %pad_maximum_fusion.refs_0_), channel_id=1, source_target_pairs={{0,24},{1,25},{2,26},{3,27},{4,28},{5,29},{6,30},{7,31},{8,16},{9,... | collective-permute-start | bytes 245768 | tf_op jit(solution)/shard_map/ppermute | solution.py:297
  55.1 0.8 %collective-permute-start.4 = (f32[160,128]{1,0:T(8,128)S(1)}, f32[160,128]{1,0:T(8,128)S(1)}, u32[]{:S(2)}, u32[]{:S(2)}) collective-permute-start(f32[160,128]{1,0:T(8,128)S(1)} %pad_maximum_fusion.refs_0_), channel_id=1, source_target_pairs={{0,16},{1,17},{2,18},{3,19},{4,20},{5,21},{6,22},{7,23},{8,24},{9,... | collective-permute-start | bytes 245768 | tf_op jit(solution)/shard_map/ppermute | solution.py:297
  55.9 0.5 collective-permute-start.3
  56.4 0.0 collective-permute-start.6
  56.4 2.4 %collective-permute-done.5.refs_3_ = f32[160,128]{1,0:T(8,128)S(1)} collective-permute-done((f32[160,128]{1,0:T(8,128)S(1)}, f32[160,128]{1,0:T(8,128)S(1)}, u32[]{:S(2)}, u32[]{:S(2)}) %collective-permute-start.5) | collective-permute-done | bytes 81952 | tf_op jit(solution)/shard_map/ppermute | solution.py:297
  58.8 0.0 collective-permute-start.9
  58.8 2.2 %collective-permute-done.4.refs_2_ = f32[160,128]{1,0:T(8,128)S(1)} collective-permute-done((f32[160,128]{1,0:T(8,128)S(1)}, f32[160,128]{1,0:T(8,128)S(1)}, u32[]{:S(2)}, u32[]{:S(2)}) %collective-permute-start.4) | collective-permute-done | bytes 81952 | tf_op jit(solution)/shard_map/ppermute | solution.py:297
  61.0 0.0 collective-permute-start.8
  61.0 0.0 collective-permute-done.3.refs_1_
  61.0 0.5 collective-permute-start.7
  61.5 0.0 collective-permute-done.6.refs_4_
  61.5 0.0 collective-permute-done.9.refs_7_
  61.5 0.8 %collective-permute-done.8.refs_6_ = f32[160,128]{1,0:T(8,128)S(1)} collective-permute-done((f32[160,128]{1,0:T(8,128)S(1)}, f32[160,128]{1,0:T(8,128)S(1)}, u32[]{:S(2)}, u32[]{:S(2)}) %collective-permute-start.8) | collective-permute-done | bytes 81952 | tf_op jit(solution)/shard_map/ppermute | solution.py:297
  62.3 0.2 collective-permute-done.7.refs_5_
  62.4 0.0 copy-done
  62.4 2.2 %shard_map.141 = (f32[64,128]{1,0:T(8,128)}, f32[64,128]{1,0:T(8,128)S(1)}) custom-call(s32[1]{0:T(128)} %bitcast.me_ref, s32[32,128]{1,0:T(8,128)S(1)} %bitcast.14, f32[160,128]{1,0:T(8,128)S(1)} %pad_maximum_fusion.refs_0_, f32[160,128]{1,0:T(8,128)S(1)} %collective-permute-done.3.refs_1_, f32[160,128]{1,0:T(8,128)S(1)} %collective-permute-done.4.refs_2_, ...), custom_call_target="tpu_custom_call" | custom-call | tf_op jit(solution)/shard_map/pallas_call | solution.py:280
  64.6 4.1 %collective-permute-start.12 = (f32[64,128]{1,0:T(8,128)S(1)}, f32[64,128]{1,0:T(8,128)S(1)}, u32[]{:S(2)}, u32[]{:S(2)}) collective-permute-start(f32[64,128]{1,0:T(8,128)S(1)} %get-tuple-element.4), channel_id=1, source_target_pairs={{0,96},{32,64},{64,32},{96,0},{1,97},{33,65},{65,33},{97,1},{2,98}... | collective-permute-start | bytes 98312 | tf_op jit(solution)/shard_map/ppermute | solution.py:297
  68.7 0.0 collective-permute-start.11
  68.7 0.9 %collective-permute-start.10 = (f32[64,128]{1,0:T(8,128)S(1)}, f32[64,128]{1,0:T(8,128)S(1)}, u32[]{:S(2)}, u32[]{:S(2)}) collective-permute-start(f32[64,128]{1,0:T(8,128)S(1)} %get-tuple-element.4), channel_id=1, source_target_pairs={{0,32},{32,0},{64,96},{96,64},{1,33},{33,1},{65,97},{97,65},{2,34}... | collective-permute-start | bytes 98312 | tf_op jit(solution)/shard_map/ppermute | solution.py:297
  69.6 1.0 %collective-permute-done.12 = f32[64,128]{1,0:T(8,128)S(1)} collective-permute-done((f32[64,128]{1,0:T(8,128)S(1)}, f32[64,128]{1,0:T(8,128)S(1)}, u32[]{:S(2)}, u32[]{:S(2)}) %collective-permute-start.12) | collective-permute-done | bytes 32800 | tf_op jit(solution)/shard_map/ppermute | solution.py:297
  70.6 3.5 %collective-permute-done.11 = f32[64,128]{1,0:T(8,128)S(1)} collective-permute-done((f32[64,128]{1,0:T(8,128)S(1)}, f32[64,128]{1,0:T(8,128)S(1)}, u32[]{:S(2)}, u32[]{:S(2)}) %collective-permute-start.11) | collective-permute-done | bytes 32800 | tf_op jit(solution)/shard_map/ppermute | solution.py:297
  74.1 0.0 collective-permute-done.10
  74.1 0.6 add_bitcast_fusion
Async XLA Ops:
  0.6 61.8 %copy-start = (s32[4096]{0:T(1024)S(1)}, s32[4096]{0:T(1024)}, u32[]{:S(2)}) copy-start(s32[4096]{0:T(1024)} %param.17) | copy-start | bytes 49156
  43.0 5.2 %collective-permute-start.2 = (f32[40,128]{1,0:T(8,128)}, f32[40,128]{1,0:T(8,128)S(1)}, u32[]{:S(2)}, u32[]{:S(2)}) collective-permute-start(f32[40,128]{1,0:T(8,128)} %shard_map.140), channel_id=1, source_target_pairs={{0,6},{1,7},{2,4},{3,5},{4,2},{5,3},{6,0},{7,1},{8,14},{9,15},{10,... | collective-permute-start | bytes 61448 | tf_op jit(solution)/shard_map/ppermute | solution.py:297
  46.1 5.5 %collective-permute-start.1 = (f32[40,128]{1,0:T(8,128)}, f32[40,128]{1,0:T(8,128)S(1)}, u32[]{:S(2)}, u32[]{:S(2)}) collective-permute-start(f32[40,128]{1,0:T(8,128)} %shard_map.140), channel_id=1, source_target_pairs={{0,4},{1,5},{2,6},{3,7},{4,0},{5,1},{6,2},{7,3},{8,12},{9,13},{10,... | collective-permute-start | bytes 61448 | tf_op jit(solution)/shard_map/ppermute | solution.py:297
  46.7 4.9 %collective-permute-start = (f32[40,128]{1,0:T(8,128)}, f32[40,128]{1,0:T(8,128)S(1)}, u32[]{:S(2)}, u32[]{:S(2)}) collective-permute-start(f32[40,128]{1,0:T(8,128)} %shard_map.140), channel_id=1, source_target_pairs={{0,2},{1,3},{2,0},{3,1},{4,6},{5,7},{6,4},{7,5},{8,10},{9,11},{10,... | collective-permute-start | bytes 61448 | tf_op jit(solution)/shard_map/ppermute | solution.py:297
  52.3 6.5 %collective-permute-start.5 = (f32[160,128]{1,0:T(8,128)S(1)}, f32[160,128]{1,0:T(8,128)S(1)}, u32[]{:S(2)}, u32[]{:S(2)}) collective-permute-start(f32[160,128]{1,0:T(8,128)S(1)} %pad_maximum_fusion.refs_0_), channel_id=1, source_target_pairs={{0,24},{1,25},{2,26},{3,27},{4,28},{5,29},{6,30},{7,31},{8,16},{9,... | collective-permute-start | bytes 245768 | tf_op jit(solution)/shard_map/ppermute | solution.py:297
  55.1 5.9 %collective-permute-start.4 = (f32[160,128]{1,0:T(8,128)S(1)}, f32[160,128]{1,0:T(8,128)S(1)}, u32[]{:S(2)}, u32[]{:S(2)}) collective-permute-start(f32[160,128]{1,0:T(8,128)S(1)} %pad_maximum_fusion.refs_0_), channel_id=1, source_target_pairs={{0,16},{1,17},{2,18},{3,19},{4,20},{5,21},{6,22},{7,23},{8,24},{9,... | collective-permute-start | bytes 245768 | tf_op jit(solution)/shard_map/ppermute | solution.py:297
  55.9 5.1 %collective-permute-start.3 = (f32[160,128]{1,0:T(8,128)S(1)}, f32[160,128]{1,0:T(8,128)S(1)}, u32[]{:S(2)}, u32[]{:S(2)}) collective-permute-start(f32[160,128]{1,0:T(8,128)S(1)} %pad_maximum_fusion.refs_0_), channel_id=1, source_target_pairs={{0,8},{1,9},{2,10},{3,11},{4,12},{5,13},{6,14},{7,15},{8,0},{9,1},... | collective-permute-start | bytes 245768 | tf_op jit(solution)/shard_map/ppermute | solution.py:297
  56.4 5.1 %collective-permute-start.6 = (f32[160,128]{1,0:T(8,128)S(1)}, f32[160,128]{1,0:T(8,128)S(1)}, u32[]{:S(2)}, u32[]{:S(2)}) collective-permute-start(f32[160,128]{1,0:T(8,128)S(1)} %pad_maximum_fusion.refs_0_), channel_id=1, source_target_pairs={{0,1},{1,0},{2,3},{3,2},{4,5},{5,4},{6,7},{7,6},{8,9},{9,8},{10,11... | collective-permute-start | bytes 245768 | tf_op jit(solution)/shard_map/ppermute | solution.py:297
  58.8 2.7 %collective-permute-start.9 = (f32[160,128]{1,0:T(8,128)S(1)}, f32[160,128]{1,0:T(8,128)S(1)}, u32[]{:S(2)}, u32[]{:S(2)}) collective-permute-start(f32[160,128]{1,0:T(8,128)S(1)} %collective-permute-done.5.refs_3_), channel_id=1, source_target_pairs={{0,1},{1,0},{2,3},{3,2},{4,5},{5,4},{6,7},{7,6},{8,9},{9,8},{10,11... | collective-permute-start | bytes 245768 | tf_op jit(solution)/shard_map/ppermute | solution.py:297
  61.0 1.3 %collective-permute-start.8 = (f32[160,128]{1,0:T(8,128)S(1)}, f32[160,128]{1,0:T(8,128)S(1)}, u32[]{:S(2)}, u32[]{:S(2)}) collective-permute-start(f32[160,128]{1,0:T(8,128)S(1)} %collective-permute-done.4.refs_2_), channel_id=1, source_target_pairs={{0,1},{1,0},{2,3},{3,2},{4,5},{5,4},{6,7},{7,6},{8,9},{9,8},{10,11... | collective-permute-start | bytes 245768 | tf_op jit(solution)/shard_map/ppermute | solution.py:297
  61.0 1.4 %collective-permute-start.7 = (f32[160,128]{1,0:T(8,128)S(1)}, f32[160,128]{1,0:T(8,128)S(1)}, u32[]{:S(2)}, u32[]{:S(2)}) collective-permute-start(f32[160,128]{1,0:T(8,128)S(1)} %collective-permute-done.3.refs_1_), channel_id=1, source_target_pairs={{0,1},{1,0},{2,3},{3,2},{4,5},{5,4},{6,7},{7,6},{8,9},{9,8},{10,11... | collective-permute-start | bytes 245768 | tf_op jit(solution)/shard_map/ppermute | solution.py:297
  64.6 6.0 %collective-permute-start.12 = (f32[64,128]{1,0:T(8,128)S(1)}, f32[64,128]{1,0:T(8,128)S(1)}, u32[]{:S(2)}, u32[]{:S(2)}) collective-permute-start(f32[64,128]{1,0:T(8,128)S(1)} %get-tuple-element.4), channel_id=1, source_target_pairs={{0,96},{32,64},{64,32},{96,0},{1,97},{33,65},{65,33},{97,1},{2,98}... | collective-permute-start | bytes 98312 | tf_op jit(solution)/shard_map/ppermute | solution.py:297
  68.7 5.4 %collective-permute-start.11 = (f32[64,128]{1,0:T(8,128)S(1)}, f32[64,128]{1,0:T(8,128)S(1)}, u32[]{:S(2)}, u32[]{:S(2)}) collective-permute-start(f32[64,128]{1,0:T(8,128)S(1)} %get-tuple-element.4), channel_id=1, source_target_pairs={{0,64},{32,96},{64,0},{96,32},{1,65},{33,97},{65,1},{97,33},{2,66}... | collective-permute-start | bytes 98312 | tf_op jit(solution)/shard_map/ppermute | solution.py:297
  68.7 5.4 %collective-permute-start.10 = (f32[64,128]{1,0:T(8,128)S(1)}, f32[64,128]{1,0:T(8,128)S(1)}, u32[]{:S(2)}, u32[]{:S(2)}) collective-permute-start(f32[64,128]{1,0:T(8,128)S(1)} %get-tuple-element.4), channel_id=1, source_target_pairs={{0,32},{32,0},{64,96},{96,64},{1,33},{33,1},{65,97},{97,65},{2,34}... | collective-permute-start | bytes 98312 | tf_op jit(solution)/shard_map/ppermute | solution.py:297

commit v3 on v2

--- a/solution.py
+++ b/solution.py
@@ -47,18 +47,31 @@
             ws_ref[:, at : at + 128] = jnp.concatenate(cols, axis=1)
 
 
-def kernel(sites, corners, vol, sw, sb, w1, b1, w2, b2, hw, hb, dest, ids, out, vf, ub, taps, pf0, pf1, pq1, pq2, ws, big1, big2, acc):
-    def widen(z, c):
-        vf[z] = vol[z].astype(F32)
-        return c
-
-    lax.fori_loop(0, 128, widen, 0)
-    toeplitz(w1, big1)
-    toeplitz(w2, big2)
+def kernel(sites, corners, vol, sw, sb, w1, b1, w2, b2, hw, hb, dest, ids, out, vf, ub, taps, pf0, pf1, pq1, pq2, ws, big1, big2, acc, vb, wa, wb, sems):
+    copies = [
+        pltpu.make_async_copy(vol.at[pl.ds(16 * c, 16)], vb.at[pl.ds(16 * c, 16)], sems.at[c]) for c in range(8)
+    ]
+    copies += [pltpu.make_async_copy(w1, wa, sems.at[8]), pltpu.make_async_copy(w2, wb, sems.at[9])]
+    for copy in copies:
+        copy.start()
     taps[...] = jnp.zeros_like(taps)
     for j in range(9):
         taps[3 * j : 3 * j + 3, :] = sw[j].astype(F32)
     stem_weights(taps[...].astype(BF16), ws)
+    for c in range(8):
+        copies[c].wait()
+
+        def widen(i, carry, c=c):
+            for k in range(8):
+                z = 16 * c + 8 * i + k
+                vf[z] = vb[z].astype(F32)
+            return carry
+
+        lax.fori_loop(0, 2, widen, 0)
+    copies[8].wait()
+    toeplitz(wa, big1)
+    copies[9].wait()
+    toeplitz(wb, big2)
 
     lane = lanes_of((16, 128))
     masks = [[lane < STEP * (j + 1) + 16 * h for j in range(5)] for h in range(2)]
@@ -120,39 +133,39 @@
                 pq1[z, x, p, at, 0:128] = v[p]
                 pq1[z, x, p, at, 128:256] = q[p]
 
-    build(0, 0)
-    build(1, 1)
+    for t in range(4):
+        build(t, t)
     pfs = (pf0, pf1)
     for group in range(sites // GROUP):
         pf, done = pfs[group % 2], pfs[(group + 1) % 2]
 
-        def four(i, c, group=group, pf=pf, done=done):
-            s = group * GROUP + 4 * i
-            build(s + 2, 2)
-            build(s + 3, 3)
-            stem(pf, 4 * i, (0, 1))
-            if group > 0:
-                pack(done, 2 * i, group - 1)
-                pack(done, 2 * i + 1, group - 1)
-            build(jnp.minimum(s + 4, sites - 1), 0)
-            build(jnp.minimum(s + 5, sites - 1), 1)
-            stem(pf, 4 * i + 2, (2, 3))
+        def eight(i, c, group=group, pf=pf, done=done):
+            s = group * GROUP + 8 * i
+            for part in range(2):
+                for t in range(4):
+                    build(jnp.minimum(s + 4 * part + 4 + t, sites - 1), 4 * (1 - part) + t)
+                for t in (0, 2):
+                    stem(pf, 8 * i + 4 * part + t, (4 * part + t, 4 * part + t + 1))
+                if group > 0:
+                    for z in range(2):
+                        pack(done, 4 * i + 2 * part + z, group - 1)
             return c
 
-        lax.fori_loop(0, GROUP // 4, four, 0)
+        lax.fori_loop(0, GROUP // 8, eight, 0)
 
     def last(z, c):
         pack(pfs[(sites // GROUP - 1) % 2], z, sites // GROUP - 1)
         return c
 
-    lax.fori_loop(0, 8, last, 0)
-
-    def conv(src, big, z, dzs, xb):
+    for z in range(8):
+        last(z, 0)
+
+    def conv(src, big, z, dzs, xb, nz):
         xis = [xi for xi in range(4) if 0 <= 2 * xb - 1 + xi < 8]
         total = None
         for dz in dzs:
             for xi in xis:
-                lhs = src[z + dz - 1, 2 * xb - 1 + xi].reshape(4 * sites, 256)
+                lhs = src[pl.ds(z + dz - 1, nz), 2 * xb - 1 + xi].reshape(nz * 4 * sites, 256)
                 part = jnp.dot(lhs, big[dz * 4 + xi], preferred_element_type=F32)
                 total = part if total is None else total + part
         return total
@@ -160,27 +173,31 @@
     bias1 = jnp.concatenate([b1[...]] * 4, axis=1)
     bias2 = jnp.concatenate([b2[...]] * 4, axis=1)
 
-    def first(z, dzs):
+    def first(z, dzs, nz):
         for xb in range(4):
-            v = jnp.maximum(conv(pq1, big1, z, dzs, xb) + bias1, 0.0).reshape(4, sites, 256)
-            for xo in range(2):
-                t = [v[p, :, xo * 128 : xo * 128 + 128].astype(BF16) for p in range(4)]
-                q = halo(t, low)
-                for p in range(4):
-                    pq2[z, 2 * xb + xo, p, :, 0:128] = t[p]
-                    pq2[z, 2 * xb + xo, p, :, 128:256] = q[p]
-
-    def second(z, dzs):
+            v = jnp.maximum(conv(pq1, big1, z, dzs, xb, nz) + bias1, 0.0).reshape(nz, 4, sites, 256)
+            for k in range(nz):
+                for xo in range(2):
+                    t = [v[k, p, :, xo * 128 : xo * 128 + 128].astype(BF16) for p in range(4)]
+                    q = halo(t, low)
+                    for p in range(4):
+                        pq2[z + k, 2 * xb + xo, p, :, 0:128] = t[p]
+                        pq2[z + k, 2 * xb + xo, p, :, 128:256] = q[p]
+
+    def second(z, dzs, nz):
         for xb in range(4):
-            v = conv(pq2, big2, z, dzs, xb) + bias2
-            skip = jnp.concatenate([pq1[z, 2 * xb + xo, :, :, 0:128].reshape(4 * sites, 128) for xo in range(2)], axis=1)
-            v = jnp.maximum(v + skip.astype(F32), 0.0).reshape(4, sites, 256)
+            v = conv(pq2, big2, z, dzs, xb, nz) + bias2
+            skip = jnp.concatenate(
+                [pq1[pl.ds(z, nz), 2 * xb + xo, :, :, 0:128].reshape(nz * 4 * sites, 128) for xo in range(2)], axis=1
+            )
+            v = jnp.maximum(v + skip.astype(F32), 0.0).reshape(nz * 4, sites, 256)
             acc[...] += jnp.sum(v, axis=0)
 
     def over_z(step):
-        step(0, (1, 2))
-        lax.fori_loop(1, 7, lambda z, c: (step(z, (0, 1, 2)), c)[1], 0)
-        step(7, (0, 1))
+        step(0, (1, 2), 1)
+        step(1, (0, 1, 2), 3)
+        step(4, (0, 1, 2), 3)
+        step(7, (0, 1), 1)
 
     over_z(first)
     acc[...] = jnp.zeros_like(acc)
@@ -198,15 +215,16 @@
     sites = corners.shape[1]
     sw = stem_w.transpose(0, 1, 3, 2, 4).reshape(9, 3, 64)
     vmem = pl.BlockSpec(memory_space=pltpu.VMEM)
+    hbm = pl.BlockSpec(memory_space=pl.ANY)
     smem = pl.BlockSpec(memory_space=pltpu.SMEM)
     return pl.pallas_call(
         functools.partial(kernel, sites),
         out_shape=jax.ShapeDtypeStruct((sites // 2 + 8, 128), F32),
-        in_specs=[smem] + [vmem] * 11,
+        in_specs=[smem, hbm, vmem, vmem, hbm, vmem, hbm] + [vmem] * 5,
         out_specs=vmem,
         scratch_shapes=[
             pltpu.VMEM((128, 128, 128), F32),
-            pltpu.VMEM((4, 2, 17, 16, 128), BF16),
+            pltpu.VMEM((8, 2, 17, 16, 128), BF16),
             pltpu.VMEM((32, 64), F32),
             pltpu.VMEM((8, 4, 8 * (GROUP + 1), 128), F32),
             pltpu.VMEM((8, 4, 8 * (GROUP + 1), 128), F32),
@@ -216,8 +234,12 @@
             pltpu.VMEM((12, 256, 256), BF16),
             pltpu.VMEM((12, 256, 256), BF16),
             pltpu.VMEM((sites, 256), F32),
+            pltpu.VMEM((128, 128, 128), BF16),
+            pltpu.VMEM((27, 64, 64), BF16),
+            pltpu.VMEM((27, 64, 64), BF16),
+            pltpu.SemaphoreType.DMA((10,)),
         ],
-        compiler_params=pltpu.CompilerParams(vmem_limit_bytes=56 * 1024 * 1024),
+        compiler_params=pltpu.CompilerParams(vmem_limit_bytes=60 * 1024 * 1024),
         cost_estimate=pl.CostEstimate(flops=30_000_000_000, bytes_accessed=6_000_000, transcendentals=0),
     )(
         corners, volume, sw, stem_b.reshape(1, 64), conv_w1.reshape(27, 64, 64), conv_b1.reshape(1, 64),

time: 74.9 us -> 70.4 us (0.940)
  Pallas kernels: 44.5 us -> 39.8 us
    pallas_call x1, Pallas kernels: 42.3 us -> 37.6 us  [embed(): pl.pallas_call(functools.partial(kernel, sites), out_shape=jax.ShapeDtype...]
where the time goes in v3:
time: 70.4 us; the launch traced here: 70.1 us
  Pallas kernels  39.8 us (57%)
  waiting for transfers between devices  14.6 us (21%)
  starting transfers between devices  13.7 us (19%)
  other arithmetic  1.36 us (2%)
    pallas_call x1, Pallas kernels, embed(): pl.pallas_call(functools.partial(kernel, sites), out_shape=jax.ShapeDtype...  37.6 us
    ppermute x13, waiting for transfers between devices, swap(): return lax.ppermute(a, axis, [(i, i ^ k) for i in range(n)])  14.6 us
    ppermute x13, starting transfers between devices, swap(): return lax.ppermute(a, axis, [(i, i ^ k) for i in range(n)])  13.7 us
    pallas_call x1, Pallas kernels, collect(): pl.pallas_call(functools.partial(collect_kernel, n_xy, own_rows, source_o...  2.19 us
  transfers between devices with their start and end apart: 13, of which 8 were waited for; matrix products, arithmetic and copies ran while one was open for 0% of the time, Pallas kernels for 0%

profile of v3, /device:TPU:0, one launch (start us, length us, event | category | flops | bytes accessed | tf_op | source)
XLA Modules:
  0.0 70.1 jit_solution(17261023666600342555)
XLA Ops:
  0.6 0.0 copy-start
  0.6 37.6 %shard_map.140 = f32[40,128]{1,0:T(8,128)} custom-call(s32[3,64]{1,0:T(4,128)} %corners.1, bf16[128,128,128]{2,1,0:T(8,128)(2,1)} %vol.1, bf16[9,3,64]{2,1,0:T(4,128)(2,1)} %bitcast.18, f32[1,64]{1,0:T(1,128)} %bitcast.19, bf16[27,64,64]{2,1,0:T(8,128)(2,1)} %bitcast.15, f32[1,64]{1,0:T(1,128)} %bitcast.20, bf16[27,64,64]{2,1,0:T(8,128)(2,1)} %bitcast.16, ...), custom_call_target="tpu_custom_call" | custom-call | flops 30000001024 | bytes 6000000 | tf_op jit(solution)/shard_map/pallas_call | solution.py:220
  38.3 3.2 %collective-permute-start.2 = (f32[40,128]{1,0:T(8,128)}, f32[40,128]{1,0:T(8,128)S(1)}, u32[]{:S(2)}, u32[]{:S(2)}) collective-permute-start(f32[40,128]{1,0:T(8,128)} %shard_map.140), channel_id=1, source_target_pairs={{0,6},{1,7},{2,4},{3,5},{4,2},{5,3},{6,0},{7,1},{8,14},{9,15},{10,... | collective-permute-start | bytes 61448 | tf_op jit(solution)/shard_map/ppermute | solution.py:319
  41.5 0.6 collective-permute-start.1
  42.1 0.4 collective-permute-start
  42.5 1.1 %collective-permute-done.2 = f32[40,128]{1,0:T(8,128)S(1)} collective-permute-done((f32[40,128]{1,0:T(8,128)}, f32[40,128]{1,0:T(8,128)S(1)}, u32[]{:S(2)}, u32[]{:S(2)}) %collective-permute-start.2) | collective-permute-done | bytes 20512 | tf_op jit(solution)/shard_map/ppermute | solution.py:319
  43.6 3.4 %collective-permute-done.1 = f32[40,128]{1,0:T(8,128)S(1)} collective-permute-done((f32[40,128]{1,0:T(8,128)}, f32[40,128]{1,0:T(8,128)S(1)}, u32[]{:S(2)}, u32[]{:S(2)}) %collective-permute-start.1) | collective-permute-done | bytes 20512 | tf_op jit(solution)/shard_map/ppermute | solution.py:319
  47.0 0.0 collective-permute-done
  47.0 0.7 %pad_maximum_fusion.refs_0_ = f32[160,128]{1,0:T(8,128)S(1)} fusion(f32[40,128]{1,0:T(8,128)S(1)} %collective-permute-done.2, f32[40,128]{1,0:T(8,128)S(1)} %collective-permute-done.1, f32[40,128]{1,0:T(8,128)S(1)} %collective-permute-done, f32[40,128]{1,0:T(8,128)} %shard_map.140), kind=kLoop, calls=%fused_computation | loop fusion | flops 61440 | bytes 163840 | tf_op jit(solution)/shard_map/concatenate | solution.py:324
  47.7 2.8 %collective-permute-start.5 = (f32[160,128]{1,0:T(8,128)S(1)}, f32[160,128]{1,0:T(8,128)S(1)}, u32[]{:S(2)}, u32[]{:S(2)}) collective-permute-start(f32[160,128]{1,0:T(8,128)S(1)} %pad_maximum_fusion.refs_0_), channel_id=1, source_target_pairs={{0,24},{1,25},{2,26},{3,27},{4,28},{5,29},{6,30},{7,31},{8,16},{9,... | collective-permute-start | bytes 245768 | tf_op jit(solution)/shard_map/ppermute | solution.py:319
  50.5 0.8 %collective-permute-start.4 = (f32[160,128]{1,0:T(8,128)S(1)}, f32[160,128]{1,0:T(8,128)S(1)}, u32[]{:S(2)}, u32[]{:S(2)}) collective-permute-start(f32[160,128]{1,0:T(8,128)S(1)} %pad_maximum_fusion.refs_0_), channel_id=1, source_target_pairs={{0,16},{1,17},{2,18},{3,19},{4,20},{5,21},{6,22},{7,23},{8,24},{9,... | collective-permute-start | bytes 245768 | tf_op jit(solution)/shard_map/ppermute | solution.py:319
  51.3 0.5 collective-permute-start.3
  51.8 0.0 collective-permute-start.6
  51.8 2.4 %collective-permute-done.5.refs_3_ = f32[160,128]{1,0:T(8,128)S(1)} collective-permute-done((f32[160,128]{1,0:T(8,128)S(1)}, f32[160,128]{1,0:T(8,128)S(1)}, u32[]{:S(2)}, u32[]{:S(2)}) %collective-permute-start.5) | collective-permute-done | bytes 81952 | tf_op jit(solution)/shard_map/ppermute | solution.py:319
  54.2 0.0 collective-permute-start.9
  54.2 2.2 %collective-permute-done.4.refs_2_ = f32[160,128]{1,0:T(8,128)S(1)} collective-permute-done((f32[160,128]{1,0:T(8,128)S(1)}, f32[160,128]{1,0:T(8,128)S(1)}, u32[]{:S(2)}, u32[]{:S(2)}) %collective-permute-start.4) | collective-permute-done | bytes 81952 | tf_op jit(solution)/shard_map/ppermute | solution.py:319
  56.4 0.0 collective-permute-start.8
  56.4 0.0 collective-permute-done.3.refs_1_
  56.4 0.5 collective-permute-start.7
  56.9 0.0 collective-permute-done.6.refs_4_
  56.9 0.0 collective-permute-done.9.refs_7_
  56.9 0.8 %collective-permute-done.8.refs_6_ = f32[160,128]{1,0:T(8,128)S(1)} collective-permute-done((f32[160,128]{1,0:T(8,128)S(1)}, f32[160,128]{1,0:T(8,128)S(1)}, u32[]{:S(2)}, u32[]{:S(2)}) %collective-permute-start.8) | collective-permute-done | bytes 81952 | tf_op jit(solution)/shard_map/ppermute | solution.py:319
  57.7 0.2 collective-permute-done.7.refs_5_
  57.9 0.0 copy-done
  57.9 2.2 %shard_map.141 = (f32[64,128]{1,0:T(8,128)}, f32[64,128]{1,0:T(8,128)S(1)}) custom-call(s32[1]{0:T(128)} %bitcast.me_ref, s32[32,128]{1,0:T(8,128)S(1)} %bitcast.14, f32[160,128]{1,0:T(8,128)S(1)} %pad_maximum_fusion.refs_0_, f32[160,128]{1,0:T(8,128)S(1)} %collective-permute-done.3.refs_1_, f32[160,128]{1,0:T(8,128)S(1)} %collective-permute-done.4.refs_2_, ...), custom_call_target="tpu_custom_call" | custom-call | tf_op jit(solution)/shard_map/pallas_call | solution.py:302
  60.0 4.0 %collective-permute-start.12 = (f32[64,128]{1,0:T(8,128)S(1)}, f32[64,128]{1,0:T(8,128)S(1)}, u32[]{:S(2)}, u32[]{:S(2)}) collective-permute-start(f32[64,128]{1,0:T(8,128)S(1)} %get-tuple-element.4), channel_id=1, source_target_pairs={{0,96},{32,64},{64,32},{96,0},{1,97},{33,65},{65,33},{97,1},{2,98}... | collective-permute-start | bytes 98312 | tf_op jit(solution)/shard_map/ppermute | solution.py:319
  64.1 0.0 collective-permute-start.11
  64.1 0.9 %collective-permute-start.10 = (f32[64,128]{1,0:T(8,128)S(1)}, f32[64,128]{1,0:T(8,128)S(1)}, u32[]{:S(2)}, u32[]{:S(2)}) collective-permute-start(f32[64,128]{1,0:T(8,128)S(1)} %get-tuple-element.4), channel_id=1, source_target_pairs={{0,32},{32,0},{64,96},{96,64},{1,33},{33,1},{65,97},{97,65},{2,34}... | collective-permute-start | bytes 98312 | tf_op jit(solution)/shard_map/ppermute | solution.py:319
  64.9 1.0 %collective-permute-done.12 = f32[64,128]{1,0:T(8,128)S(1)} collective-permute-done((f32[64,128]{1,0:T(8,128)S(1)}, f32[64,128]{1,0:T(8,128)S(1)}, u32[]{:S(2)}, u32[]{:S(2)}) %collective-permute-start.12) | collective-permute-done | bytes 32800 | tf_op jit(solution)/shard_map/ppermute | solution.py:319
  66.0 3.5 %collective-permute-done.11 = f32[64,128]{1,0:T(8,128)S(1)} collective-permute-done((f32[64,128]{1,0:T(8,128)S(1)}, f32[64,128]{1,0:T(8,128)S(1)}, u32[]{:S(2)}, u32[]{:S(2)}) %collective-permute-start.11) | collective-permute-done | bytes 32800 | tf_op jit(solution)/shard_map/ppermute | solution.py:319
  69.5 0.0 collective-permute-done.10
  69.5 0.6 add_bitcast_fusion
Async XLA Ops:
  0.6 57.2 %copy-start = (s32[4096]{0:T(1024)S(1)}, s32[4096]{0:T(1024)}, u32[]{:S(2)}) copy-start(s32[4096]{0:T(1024)} %param.17) | copy-start | bytes 49156
  38.3 5.3 %collective-permute-start.2 = (f32[40,128]{1,0:T(8,128)}, f32[40,128]{1,0:T(8,128)S(1)}, u32[]{:S(2)}, u32[]{:S(2)}) collective-permute-start(f32[40,128]{1,0:T(8,128)} %shard_map.140), channel_id=1, source_target_pairs={{0,6},{1,7},{2,4},{3,5},{4,2},{5,3},{6,0},{7,1},{8,14},{9,15},{10,... | collective-permute-start | bytes 61448 | tf_op jit(solution)/shard_map/ppermute | solution.py:319
  41.5 5.5 %collective-permute-start.1 = (f32[40,128]{1,0:T(8,128)}, f32[40,128]{1,0:T(8,128)S(1)}, u32[]{:S(2)}, u32[]{:S(2)}) collective-permute-start(f32[40,128]{1,0:T(8,128)} %shard_map.140), channel_id=1, source_target_pairs={{0,4},{1,5},{2,6},{3,7},{4,0},{5,1},{6,2},{7,3},{8,12},{9,13},{10,... | collective-permute-start | bytes 61448 | tf_op jit(solution)/shard_map/ppermute | solution.py:319
  42.1 4.9 %collective-permute-start = (f32[40,128]{1,0:T(8,128)}, f32[40,128]{1,0:T(8,128)S(1)}, u32[]{:S(2)}, u32[]{:S(2)}) collective-permute-start(f32[40,128]{1,0:T(8,128)} %shard_map.140), channel_id=1, source_target_pairs={{0,2},{1,3},{2,0},{3,1},{4,6},{5,7},{6,4},{7,5},{8,10},{9,11},{10,... | collective-permute-start | bytes 61448 | tf_op jit(solution)/shard_map/ppermute | solution.py:319
  47.7 6.5 %collective-permute-start.5 = (f32[160,128]{1,0:T(8,128)S(1)}, f32[160,128]{1,0:T(8,128)S(1)}, u32[]{:S(2)}, u32[]{:S(2)}) collective-permute-start(f32[160,128]{1,0:T(8,128)S(1)} %pad_maximum_fusion.refs_0_), channel_id=1, source_target_pairs={{0,24},{1,25},{2,26},{3,27},{4,28},{5,29},{6,30},{7,31},{8,16},{9,... | collective-permute-start | bytes 245768 | tf_op jit(solution)/shard_map/ppermute | solution.py:319
  50.5 5.9 %collective-permute-start.4 = (f32[160,128]{1,0:T(8,128)S(1)}, f32[160,128]{1,0:T(8,128)S(1)}, u32[]{:S(2)}, u32[]{:S(2)}) collective-permute-start(f32[160,128]{1,0:T(8,128)S(1)} %pad_maximum_fusion.refs_0_), channel_id=1, source_target_pairs={{0,16},{1,17},{2,18},{3,19},{4,20},{5,21},{6,22},{7,23},{8,24},{9,... | collective-permute-start | bytes 245768 | tf_op jit(solution)/shard_map/ppermute | solution.py:319
  51.3 5.2 %collective-permute-start.3 = (f32[160,128]{1,0:T(8,128)S(1)}, f32[160,128]{1,0:T(8,128)S(1)}, u32[]{:S(2)}, u32[]{:S(2)}) collective-permute-start(f32[160,128]{1,0:T(8,128)S(1)} %pad_maximum_fusion.refs_0_), channel_id=1, source_target_pairs={{0,8},{1,9},{2,10},{3,11},{4,12},{5,13},{6,14},{7,15},{8,0},{9,1},... | collective-permute-start | bytes 245768 | tf_op jit(solution)/shard_map/ppermute | solution.py:319
  51.8 5.1 %collective-permute-start.6 = (f32[160,128]{1,0:T(8,128)S(1)}, f32[160,128]{1,0:T(8,128)S(1)}, u32[]{:S(2)}, u32[]{:S(2)}) collective-permute-start(f32[160,128]{1,0:T(8,128)S(1)} %pad_maximum_fusion.refs_0_), channel_id=1, source_target_pairs={{0,1},{1,0},{2,3},{3,2},{4,5},{5,4},{6,7},{7,6},{8,9},{9,8},{10,11... | collective-permute-start | bytes 245768 | tf_op jit(solution)/shard_map/ppermute | solution.py:319
  54.2 2.7 %collective-permute-start.9 = (f32[160,128]{1,0:T(8,128)S(1)}, f32[160,128]{1,0:T(8,128)S(1)}, u32[]{:S(2)}, u32[]{:S(2)}) collective-permute-start(f32[160,128]{1,0:T(8,128)S(1)} %collective-permute-done.5.refs_3_), channel_id=1, source_target_pairs={{0,1},{1,0},{2,3},{3,2},{4,5},{5,4},{6,7},{7,6},{8,9},{9,8},{10,11... | collective-permute-start | bytes 245768 | tf_op jit(solution)/shard_map/ppermute | solution.py:319
  56.4 1.3 %collective-permute-start.8 = (f32[160,128]{1,0:T(8,128)S(1)}, f32[160,128]{1,0:T(8,128)S(1)}, u32[]{:S(2)}, u32[]{:S(2)}) collective-permute-start(f32[160,128]{1,0:T(8,128)S(1)} %collective-permute-done.4.refs_2_), channel_id=1, source_target_pairs={{0,1},{1,0},{2,3},{3,2},{4,5},{5,4},{6,7},{7,6},{8,9},{9,8},{10,11... | collective-permute-start | bytes 245768 | tf_op jit(solution)/shard_map/ppermute | solution.py:319
  56.4 1.4 %collective-permute-start.7 = (f32[160,128]{1,0:T(8,128)S(1)}, f32[160,128]{1,0:T(8,128)S(1)}, u32[]{:S(2)}, u32[]{:S(2)}) collective-permute-start(f32[160,128]{1,0:T(8,128)S(1)} %collective-permute-done.3.refs_1_), channel_id=1, source_target_pairs={{0,1},{1,0},{2,3},{3,2},{4,5},{5,4},{6,7},{7,6},{8,9},{9,8},{10,11... | collective-permute-start | bytes 245768 | tf_op jit(solution)/shard_map/ppermute | solution.py:319
  60.0 5.9 %collective-permute-start.12 = (f32[64,128]{1,0:T(8,128)S(1)}, f32[64,128]{1,0:T(8,128)S(1)}, u32[]{:S(2)}, u32[]{:S(2)}) collective-permute-start(f32[64,128]{1,0:T(8,128)S(1)} %get-tuple-element.4), channel_id=1, source_target_pairs={{0,96},{32,64},{64,32},{96,0},{1,97},{33,65},{65,33},{97,1},{2,98}... | collective-permute-start | bytes 98312 | tf_op jit(solution)/shard_map/ppermute | solution.py:319
  64.1 5.4 %collective-permute-start.11 = (f32[64,128]{1,0:T(8,128)S(1)}, f32[64,128]{1,0:T(8,128)S(1)}, u32[]{:S(2)}, u32[]{:S(2)}) collective-permute-start(f32[64,128]{1,0:T(8,128)S(1)} %get-tuple-element.4), channel_id=1, source_target_pairs={{0,64},{32,96},{64,0},{96,32},{1,65},{33,97},{65,1},{97,33},{2,66}... | collective-permute-start | bytes 98312 | tf_op jit(solution)/shard_map/ppermute | solution.py:319
  64.1 5.4 %collective-permute-start.10 = (f32[64,128]{1,0:T(8,128)S(1)}, f32[64,128]{1,0:T(8,128)S(1)}, u32[]{:S(2)}, u32[]{:S(2)}) collective-permute-start(f32[64,128]{1,0:T(8,128)S(1)} %get-tuple-element.4), channel_id=1, source_target_pairs={{0,32},{32,0},{64,96},{96,64},{1,33},{33,1},{65,97},{97,65},{2,34}... | collective-permute-start | bytes 98312 | tf_op jit(solution)/shard_map/ppermute | solution.py:319

commit v4 on v3

--- a/solution.py
+++ b/solution.py
@@ -28,6 +28,15 @@
                 else:
                     tile = jnp.zeros((256, 128), BF16)
                 big_ref[dz * 4 + xi, :, xo * 128 : (xo + 1) * 128] = tile
+
+
+def owned_ids(table, me, rows):
+    want = lax.broadcasted_iota(jnp.int32, (rows, 128), 0) + me * rows
+    lane = lanes_of((rows, 128))
+    found = jnp.zeros((rows, 128), jnp.int32)
+    for r in range(table.shape[0]):
+        found = found + jnp.where(table[r : r + 1, :] == want, lane + r * 128, 0)
+    return jnp.broadcast_to(jnp.sum(found, axis=1, keepdims=True), (rows, 128))
 
 
 def stem_weights(taps, ws_ref):
@@ -47,13 +56,14 @@
             ws_ref[:, at : at + 128] = jnp.concatenate(cols, axis=1)
 
 
-def kernel(sites, corners, vol, sw, sb, w1, b1, w2, b2, hw, hb, dest, ids, out, vf, ub, taps, pf0, pf1, pq1, pq2, ws, big1, big2, acc, vb, wa, wb, sems):
+def kernel(sites, corners, vol, sw, sb, w1, b1, w2, b2, hw, hb, dest, ids, me_ref, table, out, owned, vf, ub, taps, pf0, pf1, pq1, pq2, ws, big1, big2, acc, vb, wa, wb, sems):
     copies = [
         pltpu.make_async_copy(vol.at[pl.ds(16 * c, 16)], vb.at[pl.ds(16 * c, 16)], sems.at[c]) for c in range(8)
     ]
     copies += [pltpu.make_async_copy(w1, wa, sems.at[8]), pltpu.make_async_copy(w2, wb, sems.at[9])]
     for copy in copies:
         copy.start()
+    owned[...] = owned_ids(table[...], me_ref[0], owned.shape[0])
     taps[...] = jnp.zeros_like(taps)
     for j in range(9):
         taps[3 * j : 3 * j + 3, :] = sw[j].astype(F32)
@@ -64,7 +74,7 @@
         def widen(i, carry, c=c):
             for k in range(8):
                 z = 16 * c + 8 * i + k
-                vf[z] = vb[z].astype(F32)
+                vf[z, 0:128, :] = vb[z].astype(F32)
             return carry
 
         lax.fori_loop(0, 2, widen, 0)
@@ -211,7 +221,7 @@
     out[half : half + 8, :] = jnp.broadcast_to(names, (8, 128))
 
 
-def embed(volume, corners, destination, svx_ids, stem_w, stem_b, conv_w1, conv_b1, conv_w2, conv_b2, head_w, head_b):
+def embed(me, table, own_rows, volume, corners, destination, svx_ids, stem_w, stem_b, conv_w1, conv_b1, conv_w2, conv_b2, head_w, head_b):
     sites = corners.shape[1]
     sw = stem_w.transpose(0, 1, 3, 2, 4).reshape(9, 3, 64)
     vmem = pl.BlockSpec(memory_space=pltpu.VMEM)
@@ -219,15 +229,18 @@
     smem = pl.BlockSpec(memory_space=pltpu.SMEM)
     return pl.pallas_call(
         functools.partial(kernel, sites),
-        out_shape=jax.ShapeDtypeStruct((sites // 2 + 8, 128), F32),
-        in_specs=[smem, hbm, vmem, vmem, hbm, vmem, hbm] + [vmem] * 5,
-        out_specs=vmem,
+        out_shape=(
+            jax.ShapeDtypeStruct((sites // 2 + 8, 128), F32),
+            jax.ShapeDtypeStruct((own_rows, 128), jnp.int32),
+        ),
+        in_specs=[smem, hbm, vmem, vmem, hbm, vmem, hbm] + [vmem] * 5 + [smem, vmem],
+        out_specs=(vmem, vmem),
         scratch_shapes=[
-            pltpu.VMEM((128, 128, 128), F32),
+            pltpu.VMEM((128, 136, 128), F32),
             pltpu.VMEM((8, 2, 17, 16, 128), BF16),
             pltpu.VMEM((32, 64), F32),
-            pltpu.VMEM((8, 4, 8 * (GROUP + 1), 128), F32),
-            pltpu.VMEM((8, 4, 8 * (GROUP + 1), 128), F32),
+            pltpu.VMEM((8, 4, 8 * (GROUP + 1) + GROUP, 128), F32),
+            pltpu.VMEM((8, 4, 8 * (GROUP + 1) + GROUP, 128), F32),
             pltpu.VMEM((8, 8, 4, sites, 256), BF16),
             pltpu.VMEM((8, 8, 4, sites, 256), BF16),
             pltpu.VMEM((256, 1024), BF16),
@@ -244,11 +257,11 @@
     )(
         corners, volume, sw, stem_b.reshape(1, 64), conv_w1.reshape(27, 64, 64), conv_b1.reshape(1, 64),
         conv_w2.reshape(27, 64, 64), conv_b2.reshape(1, 64), head_w, head_b.reshape(1, 64),
-        destination.reshape(1, sites), svx_ids.reshape(1, sites),
+        destination.reshape(1, sites), svx_ids.reshape(1, sites), me, table,
     )
 
 
-def collect_kernel(n_xy, own_rows, source_of, me_ref, table, *refs):
+def collect_kernel(n_xy, own_rows, source_of, me_ref, owned_ref, *refs):
     pieces, (batch, sums, hots) = refs[:-3], refs[-3:]
     me = me_ref[0]
     size = pieces[0].shape[0]
@@ -260,13 +273,7 @@
     rank = jnp.dot(valid, earlier, preferred_element_type=F32).astype(jnp.int32)
     source = jnp.concatenate([jnp.full((1, 64), k, jnp.int32) for k in source_of], axis=0)
     row = jnp.where(dest == me, jnp.bitwise_xor(source, me) * 4 + rank, -1)
-    t = table[...]
-    want = lax.broadcasted_iota(jnp.int32, (own_rows, 128), 0) + me * own_rows
-    found = jnp.zeros((own_rows, 128), jnp.int32)
-    lane = lax.broadcasted_iota(jnp.int32, (own_rows, 128), 1)
-    for r in range(t.shape[0]):
-        found = found + jnp.where(t[r : r + 1, :] == want, lane + r * 128, 0)
-    owned = jnp.sum(found, axis=1, keepdims=True)
+    owned = owned_ref[...]
     rows = lax.broadcasted_iota(jnp.int32, (own_rows, 128), 0)
     for g in range(n_xy // 4):
         for half in range(2):
@@ -276,19 +283,13 @@
             at = slice(g * 128, g * 128 + 128)
             hots[top : top + own_rows, at] = (rows == w).astype(F32).astype(BF16)
             hots[top + own_rows : top + 2 * own_rows, at] = (owned == s).astype(F32).astype(BF16)
-    total = jnp.zeros((4 * own_rows, 128), F32)
-    at = 0
-    for p in pieces:
-        x = jnp.concatenate([p[r : r + 32, :] for r in range(0, size, 40)], axis=0)
-        hi = x.astype(BF16)
-        rest = x - hi.astype(F32)
-        mid = rest.astype(BF16)
-        low = (rest - mid.astype(F32)).astype(BF16)
-        parts = jnp.dot(
-            hots[:, at : at + x.shape[0]], jnp.concatenate([hi, mid, low], axis=1), preferred_element_type=F32
-        )
-        total = total + (parts[:, 0:128] + (parts[:, 128:256] + parts[:, 256:384]))
-        at += x.shape[0]
+    x = jnp.concatenate([p[r : r + 32, :] for p, r in blocks], axis=0)
+    hi = x.astype(BF16)
+    rest = x - hi.astype(F32)
+    mid = rest.astype(BF16)
+    low = (rest - mid.astype(F32)).astype(BF16)
+    total = jnp.dot(hots[...], jnp.concatenate([hi, mid, low], axis=1), preferred_element_type=F32)
+    total = total[:, 0:128] + (total[:, 128:256] + total[:, 256:384])
     n = own_rows
     both = [total[a : a + n, 0:64] + total[a + 2 * n : a + 3 * n, 64:128] for a in (0, n)]
     turned = jnp.concatenate(both, axis=1).T
@@ -296,8 +297,8 @@
     sums[...] = turned[64:128]
 
 
-def collect(pieces, source_of, table, me, n_xy):
-    own_rows = table.size // n_xy
+def collect(pieces, source_of, owned, me, n_xy):
+    own_rows = owned.shape[0]
     vmem = pl.BlockSpec(memory_space=pltpu.VMEM)
     return pl.pallas_call(
         functools.partial(collect_kernel, n_xy, own_rows, source_of),
@@ -306,7 +307,7 @@
         out_specs=(vmem, vmem),
         scratch_shapes=[pltpu.VMEM((4 * own_rows, n_xy * 32), BF16)],
         compiler_params=pltpu.CompilerParams(vmem_limit_bytes=32 * 1024 * 1024),
-    )(me, table, *pieces)
+    )(me, owned, *pieces)
 
 
 def body(
@@ -318,15 +319,15 @@
     def swap(a, k, axis="xy", n=n_xy):
         return lax.ppermute(a, axis, [(i, i ^ k) for i in range(n)])
 
-    own = embed(
-        volume, corners, destination, svx_ids, stem_w, stem_b, conv_w1, conv_b1, conv_w2, conv_b2, head_w, head_b
+    me = lax.axis_index("xy").astype(jnp.int32).reshape(1)
+    own, owned = embed(
+        me, svx_rows.reshape(-1, 128), svx_rows.size // n_xy, volume, corners, destination, svx_ids, stem_w, stem_b, conv_w1, conv_b1, conv_w2, conv_b2, head_w, head_b
     )
     a = jnp.concatenate([own] + [swap(own, k) for k in (2, 4, 6)])
     pieces = [a] + [swap(a, k) for k in (8, 16, 24)]
     pieces = pieces + [swap(p, 1) for p in pieces]
     source_of = [c + x + y for c in (0, 1) for x in (0, 8, 16, 24) for y in (0, 2, 4, 6)]
-    me = lax.axis_index("xy").astype(jnp.int32).reshape(1)
-    batch, part = collect(pieces, source_of, svx_rows.reshape(-1, 128), me, n_xy)
+    batch, part = collect(pieces, source_of, owned, me, n_xy)
     z = [part] + [swap(part, k, "gz", n_gz) for k in (1, 2, 3)]
     return ((z[0] + z[1]) + (z[2] + z[3])).T, batch.T
 

time: 70.4 us -> 70.1 us (level)
  local copies, waits for them, and re-layouts: 0.01 us -> 1.61 us
  waiting for transfers between devices: 14.6 us -> 13.8 us
  other arithmetic: 1.36 us -> 0.62 us
    unnamed x2 -> x5, local copies, waits for them, and re-layouts: 0.01 us -> 1.61 us
    ppermute x13, waiting for transfers between devices: 14.6 us -> 13.8 us  [swap(): return lax.ppermute(a, axis, [(i, i ^ k) for i in range(n)])]
    concatenate x1 -> x0, other arithmetic: 0.74 us -> none  [body(): a = jnp.concatenate([own] + [swap(own, k) for k in (2, 4, 6)])]
  transfers between devices with their start and end apart: 13 -> 13, of which waited for: 8 -> 8; matrix products, arithmetic and copies ran while one was open for 0% -> 1% of each run, Pallas kernels for 0% -> 0%
where the time goes in v4:
time: 70.1 us; the launch traced here: 69.8 us
  Pallas kernels  39.3 us (56%)
  starting transfers between devices  13.8 us (20%)
  waiting for transfers between devices  13.8 us (20%)
  local copies, waits for them, and re-layouts  1.61 us (2%)
    pallas_call x1, Pallas kernels, embed(): pl.pallas_call(functools.partial(kernel, sites), out_shape=(jax.ShapeDtyp...  37.6 us
    ppermute x13, waiting for transfers between devices, swap(): return lax.ppermute(a, axis, [(i, i ^ k) for i in range(n)])  13.8 us
    ppermute x13, starting transfers between devices, swap(): return lax.ppermute(a, axis, [(i, i ^ k) for i in range(n)])  13.8 us
    pallas_call x1, Pallas kernels, collect(): pl.pallas_call(functools.partial(collect_kernel, n_xy, own_rows, source_o...  1.71 us
    unnamed x5, local copies, waits for them, and re-layouts  1.61 us
  transfers between devices with their start and end apart: 13, of which 8 were waited for; matrix products, arithmetic and copies ran while one was open for 1% of the time, Pallas kernels for 0%

profile of v4, /device:TPU:0, one launch (start us, length us, event | category | flops | bytes accessed | tf_op | source)
XLA Modules:
  0.0 69.8 jit_solution(11590820928335459336)
XLA Ops:
  0.6 37.6 %shard_map.140 = (f32[40,128]{1,0:T(8,128)}, s32[128,128]{1,0:T(8,128)}) custom-call(s32[3,64]{1,0:T(4,128)} %corners.1, bf16[128,128,128]{2,1,0:T(8,128)(2,1)} %vol.1, bf16[9,3,64]{2,1,0:T(4,128)(2,1)} %bitcast.18, f32[1,64]{1,0:T(1,128)} %bitcast.19, bf16[27,64,64]{2,1,0:T(8,128)(2,1)} %bitcast.14, f32[1,64]{1,0:T(1,128)} %bitcast.20, ...), custom_call_target="tpu_custom_call" | custom-call | flops 30000001024 | bytes 6000000 | tf_op jit(solution)/shard_map/pallas_call | solution.py:230
  38.3 3.2 %collective-permute-start.2 = (f32[40,128]{1,0:T(8,128)}, f32[40,128]{1,0:T(8,128)S(1)}, u32[]{:S(2)}, u32[]{:S(2)}) collective-permute-start(f32[40,128]{1,0:T(8,128)} %get-tuple-element.7), channel_id=1, source_target_pairs={{0,6},{1,7},{2,4},{3,5},{4,2},{5,3},{6,0},{7,1},{8,14},{9,15},{10,... | collective-permute-start | bytes 61448 | tf_op jit(solution)/shard_map/ppermute | solution.py:320
  41.5 0.6 collective-permute-start.1
  42.1 0.4 collective-permute-start
  42.5 0.8 %constant_dynamic-update-slice_fusion.3 = f32[160,128]{1,0:T(8,128)S(1)} fusion(f32[40,128]{1,0:T(8,128)} %get-tuple-element.7), kind=kLoop, calls=%fused_computation.4 | loop fusion | bytes 40960
  43.2 2.9 %collective-permute-done = f32[40,128]{1,0:T(8,128)S(1)} collective-permute-done((f32[40,128]{1,0:T(8,128)}, f32[40,128]{1,0:T(8,128)S(1)}, u32[]{:S(2)}, u32[]{:S(2)}) %collective-permute-start) | collective-permute-done | bytes 20512 | tf_op jit(solution)/shard_map/ppermute | solution.py:320
  46.1 0.9 %collective-permute-done.1 = f32[40,128]{1,0:T(8,128)S(1)} collective-permute-done((f32[40,128]{1,0:T(8,128)}, f32[40,128]{1,0:T(8,128)S(1)}, u32[]{:S(2)}, u32[]{:S(2)}) %collective-permute-start.1) | collective-permute-done | bytes 20512 | tf_op jit(solution)/shard_map/ppermute | solution.py:320
  47.0 0.0 collective-permute-done.2
  47.0 2.8 %collective-permute-start.5 = (f32[160,128]{1,0:T(8,128)S(1)}, f32[160,128]{1,0:T(8,128)S(1)}, u32[]{:S(2)}, u32[]{:S(2)}) collective-permute-start(f32[160,128]{1,0:T(8,128)S(1)} %constant_dynamic-update-slice_fusion.refs_0_), channel_id=1, source_target_pairs={{0,24},{1,25},{2,26},{3,27},{4,28},{5,29},{6,30},{7,31},{8,16},{9,... | collective-permute-start | bytes 245768 | tf_op jit(solution)/shard_map/ppermute | solution.py:320
  49.8 0.8 %collective-permute-start.4 = (f32[160,128]{1,0:T(8,128)S(1)}, f32[160,128]{1,0:T(8,128)S(1)}, u32[]{:S(2)}, u32[]{:S(2)}) collective-permute-start(f32[160,128]{1,0:T(8,128)S(1)} %constant_dynamic-update-slice_fusion.refs_0_), channel_id=1, source_target_pairs={{0,16},{1,17},{2,18},{3,19},{4,20},{5,21},{6,22},{7,23},{8,24},{9,... | collective-permute-start | bytes 245768 | tf_op jit(solution)/shard_map/ppermute | solution.py:320
  50.6 0.5 collective-permute-start.3
  51.1 0.0 collective-permute-start.6
  51.2 2.4 %collective-permute-done.5.refs_3_ = f32[160,128]{1,0:T(8,128)S(1)} collective-permute-done((f32[160,128]{1,0:T(8,128)S(1)}, f32[160,128]{1,0:T(8,128)S(1)}, u32[]{:S(2)}, u32[]{:S(2)}) %collective-permute-start.5) | collective-permute-done | bytes 81952 | tf_op jit(solution)/shard_map/ppermute | solution.py:320
  53.6 0.0 collective-permute-start.9
  53.6 2.2 %collective-permute-done.4.refs_2_ = f32[160,128]{1,0:T(8,128)S(1)} collective-permute-done((f32[160,128]{1,0:T(8,128)S(1)}, f32[160,128]{1,0:T(8,128)S(1)}, u32[]{:S(2)}, u32[]{:S(2)}) %collective-permute-start.4) | collective-permute-done | bytes 81952 | tf_op jit(solution)/shard_map/ppermute | solution.py:320
  55.8 0.0 collective-permute-start.8
  55.8 0.0 collective-permute-done.3.refs_1_
  55.8 0.5 collective-permute-start.7
  56.3 0.0 collective-permute-done.6.refs_4_
  56.3 0.0 collective-permute-done.9.refs_7_
  56.3 0.8 %collective-permute-done.8.refs_6_ = f32[160,128]{1,0:T(8,128)S(1)} collective-permute-done((f32[160,128]{1,0:T(8,128)S(1)}, f32[160,128]{1,0:T(8,128)S(1)}, u32[]{:S(2)}, u32[]{:S(2)}) %collective-permute-start.8) | collective-permute-done | bytes 81952 | tf_op jit(solution)/shard_map/ppermute | solution.py:320
  57.0 0.2 collective-permute-done.7.refs_5_
  57.2 0.0 copy-start
  57.2 0.8 %copy-done = s32[128,128]{1,0:T(8,128)S(1)} copy-done((s32[128,128]{1,0:T(8,128)S(1)}, s32[128,128]{1,0:T(8,128)}, u32[]{:S(2)}) %copy-start) | copy-done | bytes 65560
  58.0 1.7 %shard_map.141 = (f32[64,128]{1,0:T(8,128)}, f32[64,128]{1,0:T(8,128)S(1)}) custom-call(s32[1]{0:T(128)} %bitcast.me_ref, s32[128,128]{1,0:T(8,128)S(1)} %copy-done, f32[160,128]{1,0:T(8,128)S(1)} %constant_dynamic-update-slice_fusion.refs_0_, f32[160,128]{1,0:T(8,128)S(1)} %collective-permute-done.3.refs_1_, f32[160,128]{1,0:T(8,128)S(1)} %collective-permute-done.4.refs_2_, ...), custom_call_target="tpu_custom_call" | custom-call | tf_op jit(solution)/shard_map/pallas_call | solution.py:303
  59.7 4.0 %collective-permute-start.12 = (f32[64,128]{1,0:T(8,128)S(1)}, f32[64,128]{1,0:T(8,128)S(1)}, u32[]{:S(2)}, u32[]{:S(2)}) collective-permute-start(f32[64,128]{1,0:T(8,128)S(1)} %get-tuple-element.8), channel_id=1, source_target_pairs={{0,96},{32,64},{64,32},{96,0},{1,97},{33,65},{65,33},{97,1},{2,98}... | collective-permute-start | bytes 98312 | tf_op jit(solution)/shard_map/ppermute | solution.py:320
  63.8 0.0 collective-permute-start.11
  63.8 0.9 %collective-permute-start.10 = (f32[64,128]{1,0:T(8,128)S(1)}, f32[64,128]{1,0:T(8,128)S(1)}, u32[]{:S(2)}, u32[]{:S(2)}) collective-permute-start(f32[64,128]{1,0:T(8,128)S(1)} %get-tuple-element.8), channel_id=1, source_target_pairs={{0,32},{32,0},{64,96},{96,64},{1,33},{33,1},{65,97},{97,65},{2,34}... | collective-permute-start | bytes 98312 | tf_op jit(solution)/shard_map/ppermute | solution.py:320
  64.6 1.0 %collective-permute-done.12 = f32[64,128]{1,0:T(8,128)S(1)} collective-permute-done((f32[64,128]{1,0:T(8,128)S(1)}, f32[64,128]{1,0:T(8,128)S(1)}, u32[]{:S(2)}, u32[]{:S(2)}) %collective-permute-start.12) | collective-permute-done | bytes 32800 | tf_op jit(solution)/shard_map/ppermute | solution.py:320
  65.7 3.5 %collective-permute-done.11 = f32[64,128]{1,0:T(8,128)S(1)} collective-permute-done((f32[64,128]{1,0:T(8,128)S(1)}, f32[64,128]{1,0:T(8,128)S(1)}, u32[]{:S(2)}, u32[]{:S(2)}) %collective-permute-start.11) | collective-permute-done | bytes 32800 | tf_op jit(solution)/shard_map/ppermute | solution.py:320
  69.2 0.0 collective-permute-done.10
  69.2 0.6 add_bitcast_fusion
  (3 shorter events, 0.0 us)
Async XLA Ops:
  38.3 8.7 %collective-permute-start.2 = (f32[40,128]{1,0:T(8,128)}, f32[40,128]{1,0:T(8,128)S(1)}, u32[]{:S(2)}, u32[]{:S(2)}) collective-permute-start(f32[40,128]{1,0:T(8,128)} %get-tuple-element.7), channel_id=1, source_target_pairs={{0,6},{1,7},{2,4},{3,5},{4,2},{5,3},{6,0},{7,1},{8,14},{9,15},{10,... | collective-permute-start | bytes 61448 | tf_op jit(solution)/shard_map/ppermute | solution.py:320
  41.5 5.5 %collective-permute-start.1 = (f32[40,128]{1,0:T(8,128)}, f32[40,128]{1,0:T(8,128)S(1)}, u32[]{:S(2)}, u32[]{:S(2)}) collective-permute-start(f32[40,128]{1,0:T(8,128)} %get-tuple-element.7), channel_id=1, source_target_pairs={{0,4},{1,5},{2,6},{3,7},{4,0},{5,1},{6,2},{7,3},{8,12},{9,13},{10,... | collective-permute-start | bytes 61448 | tf_op jit(solution)/shard_map/ppermute | solution.py:320
  42.1 4.0 %collective-permute-start = (f32[40,128]{1,0:T(8,128)}, f32[40,128]{1,0:T(8,128)S(1)}, u32[]{:S(2)}, u32[]{:S(2)}) collective-permute-start(f32[40,128]{1,0:T(8,128)} %get-tuple-element.7), channel_id=1, source_target_pairs={{0,2},{1,3},{2,0},{3,1},{4,6},{5,7},{6,4},{7,5},{8,10},{9,11},{10,... | collective-permute-start | bytes 61448 | tf_op jit(solution)/shard_map/ppermute | solution.py:320
  47.0 6.6 %collective-permute-start.5 = (f32[160,128]{1,0:T(8,128)S(1)}, f32[160,128]{1,0:T(8,128)S(1)}, u32[]{:S(2)}, u32[]{:S(2)}) collective-permute-start(f32[160,128]{1,0:T(8,128)S(1)} %constant_dynamic-update-slice_fusion.refs_0_), channel_id=1, source_target_pairs={{0,24},{1,25},{2,26},{3,27},{4,28},{5,29},{6,30},{7,31},{8,16},{9,... | collective-permute-start | bytes 245768 | tf_op jit(solution)/shard_map/ppermute | solution.py:320
  49.8 5.9 %collective-permute-start.4 = (f32[160,128]{1,0:T(8,128)S(1)}, f32[160,128]{1,0:T(8,128)S(1)}, u32[]{:S(2)}, u32[]{:S(2)}) collective-permute-start(f32[160,128]{1,0:T(8,128)S(1)} %constant_dynamic-update-slice_fusion.refs_0_), channel_id=1, source_target_pairs={{0,16},{1,17},{2,18},{3,19},{4,20},{5,21},{6,22},{7,23},{8,24},{9,... | collective-permute-start | bytes 245768 | tf_op jit(solution)/shard_map/ppermute | solution.py:320
  50.6 5.1 %collective-permute-start.3 = (f32[160,128]{1,0:T(8,128)S(1)}, f32[160,128]{1,0:T(8,128)S(1)}, u32[]{:S(2)}, u32[]{:S(2)}) collective-permute-start(f32[160,128]{1,0:T(8,128)S(1)} %constant_dynamic-update-slice_fusion.refs_0_), channel_id=1, source_target_pairs={{0,8},{1,9},{2,10},{3,11},{4,12},{5,13},{6,14},{7,15},{8,0},{9,1},... | collective-permute-start | bytes 245768 | tf_op jit(solution)/shard_map/ppermute | solution.py:320
  51.1 5.1 %collective-permute-start.6 = (f32[160,128]{1,0:T(8,128)S(1)}, f32[160,128]{1,0:T(8,128)S(1)}, u32[]{:S(2)}, u32[]{:S(2)}) collective-permute-start(f32[160,128]{1,0:T(8,128)S(1)} %constant_dynamic-update-slice_fusion.refs_0_), channel_id=1, source_target_pairs={{0,1},{1,0},{2,3},{3,2},{4,5},{5,4},{6,7},{7,6},{8,9},{9,8},{10,11... | collective-permute-start | bytes 245768 | tf_op jit(solution)/shard_map/ppermute | solution.py:320
  53.6 2.7 %collective-permute-start.9 = (f32[160,128]{1,0:T(8,128)S(1)}, f32[160,128]{1,0:T(8,128)S(1)}, u32[]{:S(2)}, u32[]{:S(2)}) collective-permute-start(f32[160,128]{1,0:T(8,128)S(1)} %collective-permute-done.5.refs_3_), channel_id=1, source_target_pairs={{0,1},{1,0},{2,3},{3,2},{4,5},{5,4},{6,7},{7,6},{8,9},{9,8},{10,11... | collective-permute-start | bytes 245768 | tf_op jit(solution)/shard_map/ppermute | solution.py:320
  55.8 1.3 %collective-permute-start.8 = (f32[160,128]{1,0:T(8,128)S(1)}, f32[160,128]{1,0:T(8,128)S(1)}, u32[]{:S(2)}, u32[]{:S(2)}) collective-permute-start(f32[160,128]{1,0:T(8,128)S(1)} %collective-permute-done.4.refs_2_), channel_id=1, source_target_pairs={{0,1},{1,0},{2,3},{3,2},{4,5},{5,4},{6,7},{7,6},{8,9},{9,8},{10,11... | collective-permute-start | bytes 245768 | tf_op jit(solution)/shard_map/ppermute | solution.py:320
  55.8 1.4 %collective-permute-start.7 = (f32[160,128]{1,0:T(8,128)S(1)}, f32[160,128]{1,0:T(8,128)S(1)}, u32[]{:S(2)}, u32[]{:S(2)}) collective-permute-start(f32[160,128]{1,0:T(8,128)S(1)} %collective-permute-done.3.refs_1_), channel_id=1, source_target_pairs={{0,1},{1,0},{2,3},{3,2},{4,5},{5,4},{6,7},{7,6},{8,9},{9,8},{10,11... | collective-permute-start | bytes 245768 | tf_op jit(solution)/shard_map/ppermute | solution.py:320
  57.2 0.8 %copy-start = (s32[128,128]{1,0:T(8,128)S(1)}, s32[128,128]{1,0:T(8,128)}, u32[]{:S(2)}) copy-start(s32[128,128]{1,0:T(8,128)} %get-tuple-element.6.owned_ref) | copy-start | bytes 196612
  59.7 6.0 %collective-permute-start.12 = (f32[64,128]{1,0:T(8,128)S(1)}, f32[64,128]{1,0:T(8,128)S(1)}, u32[]{:S(2)}, u32[]{:S(2)}) collective-permute-start(f32[64,128]{1,0:T(8,128)S(1)} %get-tuple-element.8), channel_id=1, source_target_pairs={{0,96},{32,64},{64,32},{96,0},{1,97},{33,65},{65,33},{97,1},{2,98}... | collective-permute-start | bytes 98312 | tf_op jit(solution)/shard_map/ppermute | solution.py:320
  63.8 5.4 %collective-permute-start.11 = (f32[64,128]{1,0:T(8,128)S(1)}, f32[64,128]{1,0:T(8,128)S(1)}, u32[]{:S(2)}, u32[]{:S(2)}) collective-permute-start(f32[64,128]{1,0:T(8,128)S(1)} %get-tuple-element.8), channel_id=1, source_target_pairs={{0,64},{32,96},{64,0},{96,32},{1,65},{33,97},{65,1},{97,33},{2,66}... | collective-permute-start | bytes 98312 | tf_op jit(solution)/shard_map/ppermute | solution.py:320
  63.8 5.4 %collective-permute-start.10 = (f32[64,128]{1,0:T(8,128)S(1)}, f32[64,128]{1,0:T(8,128)S(1)}, u32[]{:S(2)}, u32[]{:S(2)}) collective-permute-start(f32[64,128]{1,0:T(8,128)S(1)} %get-tuple-element.8), channel_id=1, source_target_pairs={{0,32},{32,0},{64,96},{96,64},{1,33},{33,1},{65,97},{97,65},{2,34}... | collective-permute-start | bytes 98312 | tf_op jit(solution)/shard_map/ppermute | solution.py:320

commit v5 on v3

--- a/solution.py
+++ b/solution.py
@@ -64,7 +64,7 @@
         def widen(i, carry, c=c):
             for k in range(8):
                 z = 16 * c + 8 * i + k
-                vf[z] = vb[z].astype(F32)
+                vf[z, 0:128, :] = vb[z].astype(F32)
             return carry
 
         lax.fori_loop(0, 2, widen, 0)
@@ -223,11 +223,11 @@
         in_specs=[smem, hbm, vmem, vmem, hbm, vmem, hbm] + [vmem] * 5,
         out_specs=vmem,
         scratch_shapes=[
-            pltpu.VMEM((128, 128, 128), F32),
+            pltpu.VMEM((128, 136, 128), F32),
             pltpu.VMEM((8, 2, 17, 16, 128), BF16),
             pltpu.VMEM((32, 64), F32),
-            pltpu.VMEM((8, 4, 8 * (GROUP + 1), 128), F32),
-            pltpu.VMEM((8, 4, 8 * (GROUP + 1), 128), F32),
+            pltpu.VMEM((8, 4, 8 * (GROUP + 1) + GROUP, 128), F32),
+            pltpu.VMEM((8, 4, 8 * (GROUP + 1) + GROUP, 128), F32),
             pltpu.VMEM((8, 8, 4, sites, 256), BF16),
             pltpu.VMEM((8, 8, 4, sites, 256), BF16),
             pltpu.VMEM((256, 1024), BF16),
@@ -276,19 +276,13 @@
             at = slice(g * 128, g * 128 + 128)
             hots[top : top + own_rows, at] = (rows == w).astype(F32).astype(BF16)
             hots[top + own_rows : top + 2 * own_rows, at] = (owned == s).astype(F32).astype(BF16)
-    total = jnp.zeros((4 * own_rows, 128), F32)
-    at = 0
-    for p in pieces:
-        x = jnp.concatenate([p[r : r + 32, :] for r in range(0, size, 40)], axis=0)
-        hi = x.astype(BF16)
-        rest = x - hi.astype(F32)
-        mid = rest.astype(BF16)
-        low = (rest - mid.astype(F32)).astype(BF16)
-        parts = jnp.dot(
-            hots[:, at : at + x.shape[0]], jnp.concatenate([hi, mid, low], axis=1), preferred_element_type=F32
-        )
-        total = total + (parts[:, 0:128] + (parts[:, 128:256] + parts[:, 256:384]))
-        at += x.shape[0]
+    x = jnp.concatenate([p[r : r + 32, :] for p, r in blocks], axis=0)
+    hi = x.astype(BF16)
+    rest = x - hi.astype(F32)
+    mid = rest.astype(BF16)
+    low = (rest - mid.astype(F32)).astype(BF16)
+    total = jnp.dot(hots[...], jnp.concatenate([hi, mid, low], axis=1), preferred_element_type=F32)
+    total = total[:, 0:128] + (total[:, 128:256] + total[:, 256:384])
     n = own_rows
     both = [total[a : a + n, 0:64] + total[a + 2 * n : a + 3 * n, 64:128] for a in (0, n)]
     turned = jnp.concatenate(both, axis=1).T

time: 70.4 us -> 70 us (level)
  no operation moved by 1% of the time
where the time goes in v5:
time: 70 us; the launch traced here: 69.8 us
  Pallas kernels  39.5 us (56%)
  waiting for transfers between devices  14.6 us (21%)
  starting transfers between devices  13.7 us (20%)
  other arithmetic  1.36 us (2%)
    pallas_call x1, Pallas kernels, embed(): pl.pallas_call(functools.partial(kernel, sites), out_shape=jax.ShapeDtype...  37.6 us
    ppermute x13, waiting for transfers between devices, swap(): return lax.ppermute(a, axis, [(i, i ^ k) for i in range(n)])  14.6 us
    ppermute x13, starting transfers between devices, swap(): return lax.ppermute(a, axis, [(i, i ^ k) for i in range(n)])  13.7 us
    pallas_call x1, Pallas kernels, collect(): pl.pallas_call(functools.partial(collect_kernel, n_xy, own_rows, source_o...  1.89 us
  transfers between devices with their start and end apart: 13, of which 8 were waited for; matrix products, arithmetic and copies ran while one was open for 0% of the time, Pallas kernels for 0%

profile of v5, /device:TPU:0, one launch (start us, length us, event | category | flops | bytes accessed | tf_op | source)
XLA Modules:
  0.0 69.8 jit_solution(5580603126306401765)
XLA Ops:
  0.6 0.0 copy-start
  0.6 37.6 %shard_map.140 = f32[40,128]{1,0:T(8,128)} custom-call(s32[3,64]{1,0:T(4,128)} %corners.1, bf16[128,128,128]{2,1,0:T(8,128)(2,1)} %vol.1, bf16[9,3,64]{2,1,0:T(4,128)(2,1)} %bitcast.18, f32[1,64]{1,0:T(1,128)} %bitcast.19, bf16[27,64,64]{2,1,0:T(8,128)(2,1)} %bitcast.15, f32[1,64]{1,0:T(1,128)} %bitcast.20, bf16[27,64,64]{2,1,0:T(8,128)(2,1)} %bitcast.16, ...), custom_call_target="tpu_custom_call" | custom-call | flops 30000001024 | bytes 6000000 | tf_op jit(solution)/shard_map/pallas_call | solution.py:220
  38.3 3.2 %collective-permute-start.2 = (f32[40,128]{1,0:T(8,128)}, f32[40,128]{1,0:T(8,128)S(1)}, u32[]{:S(2)}, u32[]{:S(2)}) collective-permute-start(f32[40,128]{1,0:T(8,128)} %shard_map.140), channel_id=1, source_target_pairs={{0,6},{1,7},{2,4},{3,5},{4,2},{5,3},{6,0},{7,1},{8,14},{9,15},{10,... | collective-permute-start | bytes 61448 | tf_op jit(solution)/shard_map/ppermute | solution.py:313
  41.4 0.6 collective-permute-start.1
  42.1 0.4 collective-permute-start
  42.4 1.1 %collective-permute-done.2 = f32[40,128]{1,0:T(8,128)S(1)} collective-permute-done((f32[40,128]{1,0:T(8,128)}, f32[40,128]{1,0:T(8,128)S(1)}, u32[]{:S(2)}, u32[]{:S(2)}) %collective-permute-start.2) | collective-permute-done | bytes 20512 | tf_op jit(solution)/shard_map/ppermute | solution.py:313
  43.5 3.4 %collective-permute-done.1 = f32[40,128]{1,0:T(8,128)S(1)} collective-permute-done((f32[40,128]{1,0:T(8,128)}, f32[40,128]{1,0:T(8,128)S(1)}, u32[]{:S(2)}, u32[]{:S(2)}) %collective-permute-start.1) | collective-permute-done | bytes 20512 | tf_op jit(solution)/shard_map/ppermute | solution.py:313
  46.9 0.0 collective-permute-done
  46.9 0.7 %pad_maximum_fusion.refs_0_ = f32[160,128]{1,0:T(8,128)S(1)} fusion(f32[40,128]{1,0:T(8,128)S(1)} %collective-permute-done.2, f32[40,128]{1,0:T(8,128)S(1)} %collective-permute-done.1, f32[40,128]{1,0:T(8,128)S(1)} %collective-permute-done, f32[40,128]{1,0:T(8,128)} %shard_map.140), kind=kLoop, calls=%fused_computation | loop fusion | flops 61440 | bytes 163840 | tf_op jit(solution)/shard_map/concatenate | solution.py:318
  47.7 2.8 %collective-permute-start.5 = (f32[160,128]{1,0:T(8,128)S(1)}, f32[160,128]{1,0:T(8,128)S(1)}, u32[]{:S(2)}, u32[]{:S(2)}) collective-permute-start(f32[160,128]{1,0:T(8,128)S(1)} %pad_maximum_fusion.refs_0_), channel_id=1, source_target_pairs={{0,24},{1,25},{2,26},{3,27},{4,28},{5,29},{6,30},{7,31},{8,16},{9,... | collective-permute-start | bytes 245768 | tf_op jit(solution)/shard_map/ppermute | solution.py:313
  50.4 0.8 %collective-permute-start.4 = (f32[160,128]{1,0:T(8,128)S(1)}, f32[160,128]{1,0:T(8,128)S(1)}, u32[]{:S(2)}, u32[]{:S(2)}) collective-permute-start(f32[160,128]{1,0:T(8,128)S(1)} %pad_maximum_fusion.refs_0_), channel_id=1, source_target_pairs={{0,16},{1,17},{2,18},{3,19},{4,20},{5,21},{6,22},{7,23},{8,24},{9,... | collective-permute-start | bytes 245768 | tf_op jit(solution)/shard_map/ppermute | solution.py:313
  51.2 0.5 collective-permute-start.3
  51.8 0.0 collective-permute-start.6
  51.8 2.4 %collective-permute-done.5.refs_3_ = f32[160,128]{1,0:T(8,128)S(1)} collective-permute-done((f32[160,128]{1,0:T(8,128)S(1)}, f32[160,128]{1,0:T(8,128)S(1)}, u32[]{:S(2)}, u32[]{:S(2)}) %collective-permute-start.5) | collective-permute-done | bytes 81952 | tf_op jit(solution)/shard_map/ppermute | solution.py:313
  54.2 0.0 collective-permute-start.9
  54.2 2.2 %collective-permute-done.4.refs_2_ = f32[160,128]{1,0:T(8,128)S(1)} collective-permute-done((f32[160,128]{1,0:T(8,128)S(1)}, f32[160,128]{1,0:T(8,128)S(1)}, u32[]{:S(2)}, u32[]{:S(2)}) %collective-permute-start.4) | collective-permute-done | bytes 81952 | tf_op jit(solution)/shard_map/ppermute | solution.py:313
  56.4 0.0 collective-permute-start.8
  56.4 0.0 collective-permute-done.3.refs_1_
  56.4 0.5 collective-permute-start.7
  56.9 0.0 collective-permute-done.6.refs_4_
  56.9 0.0 collective-permute-done.9.refs_7_
  56.9 0.8 %collective-permute-done.8.refs_6_ = f32[160,128]{1,0:T(8,128)S(1)} collective-permute-done((f32[160,128]{1,0:T(8,128)S(1)}, f32[160,128]{1,0:T(8,128)S(1)}, u32[]{:S(2)}, u32[]{:S(2)}) %collective-permute-start.8) | collective-permute-done | bytes 81952 | tf_op jit(solution)/shard_map/ppermute | solution.py:313
  57.7 0.2 collective-permute-done.7.refs_5_
  57.8 0.0 copy-done
  57.8 1.9 %shard_map.141 = (f32[64,128]{1,0:T(8,128)}, f32[64,128]{1,0:T(8,128)S(1)}) custom-call(s32[1]{0:T(128)} %bitcast.me_ref, s32[32,128]{1,0:T(8,128)S(1)} %bitcast.14, f32[160,128]{1,0:T(8,128)S(1)} %pad_maximum_fusion.refs_0_, f32[160,128]{1,0:T(8,128)S(1)} %collective-permute-done.3.refs_1_, f32[160,128]{1,0:T(8,128)S(1)} %collective-permute-done.4.refs_2_, ...), custom_call_target="tpu_custom_call" | custom-call | tf_op jit(solution)/shard_map/pallas_call | solution.py:296
  59.7 4.0 %collective-permute-start.12 = (f32[64,128]{1,0:T(8,128)S(1)}, f32[64,128]{1,0:T(8,128)S(1)}, u32[]{:S(2)}, u32[]{:S(2)}) collective-permute-start(f32[64,128]{1,0:T(8,128)S(1)} %get-tuple-element.4), channel_id=1, source_target_pairs={{0,96},{32,64},{64,32},{96,0},{1,97},{33,65},{65,33},{97,1},{2,98}... | collective-permute-start | bytes 98312 | tf_op jit(solution)/shard_map/ppermute | solution.py:313
  63.7 0.0 collective-permute-start.11
  63.7 0.9 %collective-permute-start.10 = (f32[64,128]{1,0:T(8,128)S(1)}, f32[64,128]{1,0:T(8,128)S(1)}, u32[]{:S(2)}, u32[]{:S(2)}) collective-permute-start(f32[64,128]{1,0:T(8,128)S(1)} %get-tuple-element.4), channel_id=1, source_target_pairs={{0,32},{32,0},{64,96},{96,64},{1,33},{33,1},{65,97},{97,65},{2,34}... | collective-permute-start | bytes 98312 | tf_op jit(solution)/shard_map/ppermute | solution.py:313
  64.6 1.0 %collective-permute-done.12 = f32[64,128]{1,0:T(8,128)S(1)} collective-permute-done((f32[64,128]{1,0:T(8,128)S(1)}, f32[64,128]{1,0:T(8,128)S(1)}, u32[]{:S(2)}, u32[]{:S(2)}) %collective-permute-start.12) | collective-permute-done | bytes 32800 | tf_op jit(solution)/shard_map/ppermute | solution.py:313
  65.6 3.5 %collective-permute-done.11 = f32[64,128]{1,0:T(8,128)S(1)} collective-permute-done((f32[64,128]{1,0:T(8,128)S(1)}, f32[64,128]{1,0:T(8,128)S(1)}, u32[]{:S(2)}, u32[]{:S(2)}) %collective-permute-start.11) | collective-permute-done | bytes 32800 | tf_op jit(solution)/shard_map/ppermute | solution.py:313
  69.2 0.0 collective-permute-done.10
  69.2 0.6 add_bitcast_fusion
Async XLA Ops:
  0.6 57.2 %copy-start = (s32[4096]{0:T(1024)S(1)}, s32[4096]{0:T(1024)}, u32[]{:S(2)}) copy-start(s32[4096]{0:T(1024)} %param.17) | copy-start | bytes 49156
  38.3 5.3 %collective-permute-start.2 = (f32[40,128]{1,0:T(8,128)}, f32[40,128]{1,0:T(8,128)S(1)}, u32[]{:S(2)}, u32[]{:S(2)}) collective-permute-start(f32[40,128]{1,0:T(8,128)} %shard_map.140), channel_id=1, source_target_pairs={{0,6},{1,7},{2,4},{3,5},{4,2},{5,3},{6,0},{7,1},{8,14},{9,15},{10,... | collective-permute-start | bytes 61448 | tf_op jit(solution)/shard_map/ppermute | solution.py:313
  41.4 5.5 %collective-permute-start.1 = (f32[40,128]{1,0:T(8,128)}, f32[40,128]{1,0:T(8,128)S(1)}, u32[]{:S(2)}, u32[]{:S(2)}) collective-permute-start(f32[40,128]{1,0:T(8,128)} %shard_map.140), channel_id=1, source_target_pairs={{0,4},{1,5},{2,6},{3,7},{4,0},{5,1},{6,2},{7,3},{8,12},{9,13},{10,... | collective-permute-start | bytes 61448 | tf_op jit(solution)/shard_map/ppermute | solution.py:313
  42.1 4.9 %collective-permute-start = (f32[40,128]{1,0:T(8,128)}, f32[40,128]{1,0:T(8,128)S(1)}, u32[]{:S(2)}, u32[]{:S(2)}) collective-permute-start(f32[40,128]{1,0:T(8,128)} %shard_map.140), channel_id=1, source_target_pairs={{0,2},{1,3},{2,0},{3,1},{4,6},{5,7},{6,4},{7,5},{8,10},{9,11},{10,... | collective-permute-start | bytes 61448 | tf_op jit(solution)/shard_map/ppermute | solution.py:313
  47.7 6.5 %collective-permute-start.5 = (f32[160,128]{1,0:T(8,128)S(1)}, f32[160,128]{1,0:T(8,128)S(1)}, u32[]{:S(2)}, u32[]{:S(2)}) collective-permute-start(f32[160,128]{1,0:T(8,128)S(1)} %pad_maximum_fusion.refs_0_), channel_id=1, source_target_pairs={{0,24},{1,25},{2,26},{3,27},{4,28},{5,29},{6,30},{7,31},{8,16},{9,... | collective-permute-start | bytes 245768 | tf_op jit(solution)/shard_map/ppermute | solution.py:313
  50.4 5.9 %collective-permute-start.4 = (f32[160,128]{1,0:T(8,128)S(1)}, f32[160,128]{1,0:T(8,128)S(1)}, u32[]{:S(2)}, u32[]{:S(2)}) collective-permute-start(f32[160,128]{1,0:T(8,128)S(1)} %pad_maximum_fusion.refs_0_), channel_id=1, source_target_pairs={{0,16},{1,17},{2,18},{3,19},{4,20},{5,21},{6,22},{7,23},{8,24},{9,... | collective-permute-start | bytes 245768 | tf_op jit(solution)/shard_map/ppermute | solution.py:313
  51.2 5.2 %collective-permute-start.3 = (f32[160,128]{1,0:T(8,128)S(1)}, f32[160,128]{1,0:T(8,128)S(1)}, u32[]{:S(2)}, u32[]{:S(2)}) collective-permute-start(f32[160,128]{1,0:T(8,128)S(1)} %pad_maximum_fusion.refs_0_), channel_id=1, source_target_pairs={{0,8},{1,9},{2,10},{3,11},{4,12},{5,13},{6,14},{7,15},{8,0},{9,1},... | collective-permute-start | bytes 245768 | tf_op jit(solution)/shard_map/ppermute | solution.py:313
  51.8 5.1 %collective-permute-start.6 = (f32[160,128]{1,0:T(8,128)S(1)}, f32[160,128]{1,0:T(8,128)S(1)}, u32[]{:S(2)}, u32[]{:S(2)}) collective-permute-start(f32[160,128]{1,0:T(8,128)S(1)} %pad_maximum_fusion.refs_0_), channel_id=1, source_target_pairs={{0,1},{1,0},{2,3},{3,2},{4,5},{5,4},{6,7},{7,6},{8,9},{9,8},{10,11... | collective-permute-start | bytes 245768 | tf_op jit(solution)/shard_map/ppermute | solution.py:313
  54.2 2.7 %collective-permute-start.9 = (f32[160,128]{1,0:T(8,128)S(1)}, f32[160,128]{1,0:T(8,128)S(1)}, u32[]{:S(2)}, u32[]{:S(2)}) collective-permute-start(f32[160,128]{1,0:T(8,128)S(1)} %collective-permute-done.5.refs_3_), channel_id=1, source_target_pairs={{0,1},{1,0},{2,3},{3,2},{4,5},{5,4},{6,7},{7,6},{8,9},{9,8},{10,11... | collective-permute-start | bytes 245768 | tf_op jit(solution)/shard_map/ppermute | solution.py:313
  56.4 1.3 %collective-permute-start.8 = (f32[160,128]{1,0:T(8,128)S(1)}, f32[160,128]{1,0:T(8,128)S(1)}, u32[]{:S(2)}, u32[]{:S(2)}) collective-permute-start(f32[160,128]{1,0:T(8,128)S(1)} %collective-permute-done.4.refs_2_), channel_id=1, source_target_pairs={{0,1},{1,0},{2,3},{3,2},{4,5},{5,4},{6,7},{7,6},{8,9},{9,8},{10,11... | collective-permute-start | bytes 245768 | tf_op jit(solution)/shard_map/ppermute | solution.py:313
  56.4 1.4 %collective-permute-start.7 = (f32[160,128]{1,0:T(8,128)S(1)}, f32[160,128]{1,0:T(8,128)S(1)}, u32[]{:S(2)}, u32[]{:S(2)}) collective-permute-start(f32[160,128]{1,0:T(8,128)S(1)} %collective-permute-done.3.refs_1_), channel_id=1, source_target_pairs={{0,1},{1,0},{2,3},{3,2},{4,5},{5,4},{6,7},{7,6},{8,9},{9,8},{10,11... | collective-permute-start | bytes 245768 | tf_op jit(solution)/shard_map/ppermute | solution.py:313
  59.7 5.9 %collective-permute-start.12 = (f32[64,128]{1,0:T(8,128)S(1)}, f32[64,128]{1,0:T(8,128)S(1)}, u32[]{:S(2)}, u32[]{:S(2)}) collective-permute-start(f32[64,128]{1,0:T(8,128)S(1)} %get-tuple-element.4), channel_id=1, source_target_pairs={{0,96},{32,64},{64,32},{96,0},{1,97},{33,65},{65,33},{97,1},{2,98}... | collective-permute-start | bytes 98312 | tf_op jit(solution)/shard_map/ppermute | solution.py:313
  63.7 5.4 %collective-permute-start.11 = (f32[64,128]{1,0:T(8,128)S(1)}, f32[64,128]{1,0:T(8,128)S(1)}, u32[]{:S(2)}, u32[]{:S(2)}) collective-permute-start(f32[64,128]{1,0:T(8,128)S(1)} %get-tuple-element.4), channel_id=1, source_target_pairs={{0,64},{32,96},{64,0},{96,32},{1,65},{33,97},{65,1},{97,33},{2,66}... | collective-permute-start | bytes 98312 | tf_op jit(solution)/shard_map/ppermute | solution.py:313
  63.7 5.4 %collective-permute-start.10 = (f32[64,128]{1,0:T(8,128)S(1)}, f32[64,128]{1,0:T(8,128)S(1)}, u32[]{:S(2)}, u32[]{:S(2)}) collective-permute-start(f32[64,128]{1,0:T(8,128)S(1)} %get-tuple-element.4), channel_id=1, source_target_pairs={{0,32},{32,0},{64,96},{96,64},{1,33},{33,1},{65,97},{97,65},{2,34}... | collective-permute-start | bytes 98312 | tf_op jit(solution)/shard_map/ppermute | solution.py:313
